TPU v7x, 256 devices: a whole 4x4x8 slice. The times are simulated.
256 devices in a mesh: sec: 4 (over x), ep: 64 (over y, z, core).
Axes of the slice: x: 4, y: 4, z: 8, core: 2. Of those that a mesh axis runs over, the one named last changes fastest.
Arguments:
- residual_in: bfloat16 [128, 6144], P('ep', 'sec'), may hold values from -6 to 6
- queries: bfloat16 [128, 8192], P('sec', 'ep'), may hold values from -6 to 6
- keys_new: bfloat16 [128, 8192], P('sec', 'ep'), may hold values from -6 to 6
- values_new: bfloat16 [128, 8192], P('sec', 'ep'), may hold values from -6 to 6
- cached_state: float32 [128, 64, 128, 128], P('sec', 'ep'), may hold values from -6 to 6
- incoming_state: float32 [16, 64, 128, 128], P('sec', None, 'ep'), may hold values from -6 to 6
- admit_slot: int32 [16], P('sec'), may hold values from 0 to 127, as said below
- occupancy: int32 [128], P('sec'), may hold values 0 or 1
- decay_rate: float32 [64], P('ep'), may hold values from 0.05 to 3
- out_proj: bfloat16 [8192, 6144], P('ep', 'sec'), may hold values from -0.0625 to 0.0625
- norm_gain: float32 [6144], replicated, may hold values from 0.1 to 1.9
- routes: int32 [128, 2], replicated, may hold values from 0 to 15, all different within a row; in each aligned block of 128 rows (0 to 127, 128 to 255, ...) at most 32 rows name the same one
- route_weight: float32 [128, 2], replicated, may hold values from 0.5 to 1.5
- gate_proj: bfloat16 [64, 6144, 1152], P('ep', None, 'sec'), may hold values from -0.078125 to 0.078125
- up_proj: bfloat16 [64, 6144, 1152], P('ep', None, 'sec'), may hold values from -0.078125 to 0.078125
- down_proj: bfloat16 [64, 1152, 6144], P('ep', 'sec'), may hold values from -0.09375 to 0.09375
Outputs:
- block_out: bfloat16 [128, 6144], P('ep', 'sec')
Inputs may be any that keep to these rules, and one draw needn't show every extreme that they name: `admit_slot`: requests a with a // 4 = s take distinct slots among s * 32 to (s + 1) * 32 - 1. `routes`: A row's two experts differ; at most 32 rows name any one expert, a bound that some block reaches.
All inputs are finite; a program needn't handle non-finite values. No bound on the sum of `occupancy` on one device may be relied on, other than what follows from the above.
Results may differ from a plain program's by a relative error of at most 0.017.
Values may be sent and summed in bfloat16 or wider, within the bound.
A program may use at most 128 MiB of HBM per device.

v0:
```python
import jax
import jax.numpy as jnp
from jax import lax
from jax.sharding import PartitionSpec as P

D = 6144
EXPERTS = 16


epsilon = 1e-06
exact_mode = lax.Precision.HIGHEST


def body(
    residual_in,
    queries,
    keys_new,
    values_new,
    cached_state,
    incoming_state,
    admit_slot,
    occupancy,
    decay_rate,
    out_proj,
    norm_gain,
    routes,
    route_weight,
    gate_proj,
    up_proj,
    down_proj,
):
    slot_count, heads_here, head_width, _ = cached_state.shape
    query_rows = queries.astype(jnp.float32).reshape(slot_count, heads_here, head_width)
    key_rows = keys_new.astype(jnp.float32).reshape(slot_count, heads_here, head_width)
    value_rows = values_new.astype(jnp.float32).reshape(slot_count, heads_here, head_width)
    local_slot = admit_slot % slot_count
    placing = (local_slot[None, :] == jnp.arange(slot_count, dtype=jnp.int32)[:, None]).astype(
        jnp.float32
    )
    taken_slots = jnp.sum(placing, axis=1) > 0.5
    kept_slots = occupancy.astype(jnp.float32)
    picked = jnp.einsum("sa,shk->ahk", placing, query_rows, precision=exact_mode)
    arrived_states = lax.all_to_all(
        incoming_state.astype(jnp.bfloat16), "ep", split_axis=1, concat_axis=2, tiled=True
    ).astype(incoming_state.dtype)
    arrived = jnp.einsum("ahk,ahkv->ahv", picked, arrived_states, precision=exact_mode)
    from_new = jnp.einsum("sa,ahv->shv", placing, arrived, precision=exact_mode)
    from_old = (
        jnp.einsum("shk,shkv->shv", query_rows, cached_state, precision=exact_mode)
        * kept_slots[:, None, None]
    )
    base_product = jnp.where(taken_slots[:, None, None], from_new, from_old)
    self_score = jnp.sum(query_rows * key_rows, axis=2)
    raw_output = (
        jnp.exp(-decay_rate)[None, :, None] * base_product + self_score[:, :, None] * value_rows
    )
    scaled = raw_output * lax.rsqrt(
        jnp.mean(raw_output * raw_output, axis=2, keepdims=True) + epsilon
    )
    head_out = scaled.astype(jnp.bfloat16).reshape(slot_count, heads_here * head_width)
    all_heads = lax.all_gather(head_out, "sec", axis=0, tiled=True)
    attended = lax.psum_scatter(
        jnp.dot(all_heads, out_proj, preferred_element_type=jnp.float32),
        "ep",
        scatter_dimension=0,
        tiled=True,
    )
    mixed_rows = (residual_in.astype(jnp.float32) + attended).astype(jnp.bfloat16)
    mixed_wide = mixed_rows.astype(jnp.float32)
    sec_count = lax.axis_size("sec")
    col_count = residual_in.shape[1]
    pieces = gate_proj.shape[0]
    split_count = pieces * lax.axis_size("ep") // EXPERTS
    capacity = routes.shape[0] // 4
    first_piece = lax.axis_index("ep") * pieces
    expert_ids = (first_piece + jnp.arange(pieces, dtype=jnp.int32)) // split_count
    route_hit = routes[None, :, :] == expert_ids[:, None, None]
    named_rows = jnp.any(route_hit, axis=2)
    weight = jnp.sum(jnp.where(route_hit, route_weight[None, :, :], 0.0), axis=2)
    position = jnp.cumsum(named_rows.astype(jnp.int32), axis=1) - 1
    chosen = named_rows[:, None, :] & (
        position[:, None, :] == jnp.arange(capacity, dtype=jnp.int32)[None, :, None]
    )
    pick_rows = chosen.astype(jnp.bfloat16)
    whole_rows = lax.all_gather(mixed_rows[None], ("sec", "ep"), axis=0, tiled=True)
    whole_rows = whole_rows.reshape(sec_count, -1, col_count).astype(jnp.float32)
    row_power = jnp.sum(whole_rows * whole_rows, axis=(0, 2)) / D
    gain_rows = norm_gain.reshape(sec_count, 1, col_count)
    normed = (whole_rows * lax.rsqrt(row_power + epsilon)[None, :, None] * gain_rows).astype(
        jnp.bfloat16
    )
    rows_input = jnp.einsum(
        "pkr,src->pskc", pick_rows, normed, preferred_element_type=jnp.float32
    ).astype(jnp.bfloat16)
    gate_split = gate_proj.reshape(pieces, sec_count, col_count, -1)
    up_split = up_proj.reshape(pieces, sec_count, col_count, -1)
    gate_value = jnp.einsum(
        "pskc,pscf->pkf", rows_input, gate_split, preferred_element_type=jnp.float32
    )
    up_value = jnp.einsum(
        "pskc,pscf->pkf", rows_input, up_split, preferred_element_type=jnp.float32
    )
    hidden = (jax.nn.silu(gate_value) * up_value).astype(jnp.bfloat16)
    down_split = down_proj.reshape(pieces, -1, sec_count, col_count)
    output = jnp.einsum("pkf,pfsc->pskc", hidden, down_split, preferred_element_type=jnp.float32)
    spread_weight = chosen.astype(jnp.float32) * weight[:, None, :]
    partial_terms = jnp.einsum("pkr,pskc->src", spread_weight, output, precision=exact_mode)
    routed_sum = lax.psum_scatter(
        partial_terms.reshape(-1, col_count), ("sec", "ep"), scatter_dimension=0, tiled=True
    )
    return (mixed_wide + routed_sum).astype(jnp.bfloat16)


def solution(mesh):
    in_specs = (
        P("ep", "sec"),
        P("sec", "ep"),
        P("sec", "ep"),
        P("sec", "ep"),
        P("sec", "ep", None, None),
        P("sec", None, "ep", None),
        P("sec"),
        P("sec"),
        P("ep"),
        P("ep", "sec"),
        P(),
        P(),
        P(),
        P("ep", None, "sec"),
        P("ep", None, "sec"),
        P("ep", "sec", None),
    )
    out_specs = P("ep", "sec")
    return jax.shard_map(body, mesh=mesh, in_specs=in_specs, out_specs=out_specs, check_vma=False)
```

profile of v0, /device:TPU:1, one launch (start us, length us, event | category | flops | bytes accessed | tf_op | source)
XLA Modules:
  0.0 629.9 jit_solution(13868641532991619080)
XLA Ops:
  6.5 0.0 copy-start
  6.5 0.0 copy-start.3
  6.6 0.0 copy-start.5
  6.6 1.8 copy.67
  8.4 13.2 %all-to-all-start = ((bf16[4,64,2,128]{3,2,0,1:T(2,128)(2,1)}), bf16[4,64,2,128]{3,2,0,1:T(2,128)(2,1)S(1)}, u32[]{:S(2)}, u32[]{:S(2)}) async-start(bf16[4,64,2,128]{3,2,0,1:T(2,128)(2,1)} %copy.67), calls=%async_computation | async-start | bytes 262144 | tf_op jit(solution)/shard_map/all_to_all | solution.py:43
  21.6 0.0 all-reduce.5.cloned.1.call-start
  22.3 0.7 and_select_fusion
  23.0 0.1 convert_reduce_fusion
  23.1 0.9 fusion.56
  23.9 0.8 multiply_reduce_fusion.1
  24.8 0.7 convert_element_type.80
  25.4 1.8 fusion.13
  27.2 4.7 all-to-all-done
  31.9 0.1 copy.35
  32.0 0.2 fusion.63
  32.2 0.0 copy-done.7
  32.2 0.4 multiply_reduce_fusion
  32.6 0.1 multiply_convert_fusion
  32.7 9.4 %all_gather.6 = bf16[128,128]{1,0:T(8,128)(2,1)S(1)} all-gather(bf16[32,128]{1,0:T(8,128)(2,1)S(1)} %multiply_convert_fusion), channel_id=1, replica_groups=mesh['sec'=4,'ep'=64] {'sec'}, dimensions={0}, use_global_device_ids=true | all-gather | bytes 40960 | tf_op jit(solution)/shard_map/all_gather | solution.py:61
  42.1 1.2 fusion.64
  43.2 0.0 all-reduce.5.cloned.1.call-update
  43.3 0.0 all-gather.4.cloned.1.call-start
  43.3 0.6 dynamic-slice
  44.6 179.5 %all-reduce.5.cloned.1.call-done = f32[128,1536]{1,0:T(8,128)} async-done(((f32[128,1536]{1,0:T(8,128)}), f32[128,1536]{1,0:T(8,128)}) %all-reduce.5.cloned.1.call-update) | async-done | bytes 786448
  224.1 1.4 fusion.49
  225.5 0.0 all-gather.4.cloned.1.call-update
  225.5 0.0 all-reduce.7.cloned.1.call-start
  225.7 0.1 copy.36
  225.8 6.4 %reshape.242 = bf16[4,1536,288]{1,0,2:T(4,128)(2,1)} reshape(bf16[1,6144,288]{1,2,0:T(8,128)(2,1)} %param.29) | data formatting | bytes 7077888 | tf_op jit(solution)/shard_map/reshape.34
  232.2 6.5 %reshape.243 = bf16[4,1536,288]{1,0,2:T(4,128)(2,1)} reshape(bf16[1,6144,288]{1,2,0:T(8,128)(2,1)} %param.30) | data formatting | bytes 7077888 | tf_op jit(solution)/shard_map/reshape.38
  238.7 6.5 %reshape.244 = bf16[288,4,1536]{2,1,0:T(4,128)(2,1)} reshape(bf16[1,288,6144]{2,1,0:T(8,128)(2,1)} %param.31) | data formatting | bytes 7077888 | tf_op jit(solution)/shard_map/reshape.40
  245.2 0.2 reduce-window.7
  245.3 0.1 add_reduce_fusion
  245.5 86.2 %all-gather.4.cloned.1.call-done = bf16[256,2,1536]{2,1,0:T(2,128)(2,1)} async-done(((bf16[1,2,1536]{2,1,0:T(2,128)(2,1)}), bf16[256,2,1536]{2,1,0:T(2,128)(2,1)}) %all-gather.4.cloned.1.call-update) | async-done | bytes 1572880 | tf_op jit(solution)/shard_map/all_gather | solution.py:85
  331.6 3.1 fusion.8
  334.8 0.1 reduce_sum.56
  334.9 0.1 rsqrt.20
  335.1 0.2 mul.112
  335.3 4.9 fusion.7
  340.2 4.6 convert_element_type.89
  344.8 1.7 fusion.12
  346.6 3.1 fusion.15
  349.7 5.8 fusion.9
  355.5 4.9 fusion.40
  360.4 0.0 all-reduce.7.cloned.1.call-update
  360.4 261.6 %all-reduce.7.cloned.1.call-done = f32[512,1536]{1,0:T(8,128)} async-done(((f32[512,1536]{1,0:T(8,128)}), f32[512,1536]{1,0:T(8,128)}) %all-reduce.7.cloned.1.call-update) | async-done | bytes 3145744
  622.0 0.0 copy-done.2
  622.0 1.4 fusion.48
  (22 shorter events, 0.1 us)
Async XLA Ops:
  6.5 18.9 %copy-start = (f32[32,1,128,128]{3,2,1,0:T(8,128)S(1)}, f32[32,1,128,128]{3,2,1,0:T(8,128)}, u32[]{:S(2)}) copy-start(f32[32,1,128,128]{3,2,1,0:T(8,128)} %param.20) | copy-start | bytes 6291460
  6.5 36.8 %copy-start.8 = (u32[256]{0:T(256)S(1)}, u32[256]{0:T(256)}, u32[]{:S(2)}) copy-start(u32[256]{0:T(256)} %constant.75) | copy-start | bytes 3076
  6.5 25.7 %copy-start.7 = (bf16[32,128]{1,0:T(8,128)(2,1)S(1)}, bf16[32,128]{1,0:T(8,128)(2,1)}, u32[]{:S(2)}) copy-start(bf16[32,128]{1,0:T(8,128)(2,1)} %param.19) | copy-start | bytes 24580
  6.5 35.5 %copy-start.1 = (bf16[128,1536]{1,0:T(8,128)(2,1)S(1)}, bf16[128,1536]{1,0:T(8,128)(2,1)}, u32[]{:S(2)}) copy-start(bf16[128,1536]{1,0:T(8,128)(2,1)} %param.25) | copy-start | bytes 1179652
  6.5 217.5 %copy-start.4 = (bf16[2,1536]{1,0:T(2,128)(2,1)S(1)}, bf16[2,1536]{1,0:T(2,128)(2,1)}, u32[]{:S(2)}) copy-start(bf16[2,1536]{1,0:T(2,128)(2,1)} %param.16) | copy-start | bytes 18436
  6.5 219.0 %copy-start.3 = (f32[6144]{0:T(1024)S(1)}, f32[6144]{0:T(1024)}, u32[]{:S(2)}) copy-start(f32[6144]{0:T(1024)} %param.26) | copy-start | bytes 73732
  6.6 219.1 %copy-start.5 = (s32[128,2]{0,1:T(2,128)S(1)}, s32[128,2]{0,1:T(2,128)}, u32[]{:S(2)}) copy-start(s32[128,2]{0,1:T(2,128)} %param.27) | copy-start | bytes 3076
  8.4 23.5 %all-to-all-start = ((bf16[4,64,2,128]{3,2,0,1:T(2,128)(2,1)}), bf16[4,64,2,128]{3,2,0,1:T(2,128)(2,1)S(1)}, u32[]{:S(2)}, u32[]{:S(2)}) async-start(bf16[4,64,2,128]{3,2,0,1:T(2,128)(2,1)} %copy.67), calls=%async_computation | async-start | bytes 262144 | tf_op jit(solution)/shard_map/all_to_all | solution.py:43
  21.6 202.5 %all-reduce.5.cloned.1.call-start = ((), (), s32[]{:S(2)}) async-start(), calls=%async_computation.2 | async-start | bytes 1572864
  43.3 288.4 %all-gather.4.cloned.1.call-start = ((), (), s32[]{:S(2)}) async-start(), calls=%async_computation.1 | async-start | bytes 1579008 | tf_op jit(solution)/shard_map/all_gather | solution.py:85
  225.5 396.4 %all-reduce.7.cloned.1.call-start = ((), (), s32[]{:S(2)}) async-start(), calls=%async_computation.3 | async-start | bytes 6291456
  238.7 6.6 %copy-start.6 = (f32[128,2]{0,1:T(2,128)S(1)}, f32[128,2]{0,1:T(2,128)}, u32[]{:S(2)}) copy-start(f32[128,2]{0,1:T(2,128)} %param.28) | copy-start | bytes 3076
  355.5 266.5 %copy-start.2 = (bf16[2,1536]{1,0:T(2,128)(2,1)S(1)}, bf16[2,1536]{1,0:T(2,128)(2,1)}, u32[]{:S(2)}) copy-start(bf16[2,1536]{1,0:T(2,128)(2,1)} %fusion.49) | copy-start | bytes 18436
Sparse Core Ops, SparseCore 0:
  43.4 180.6 all-reduce.4
  228.2 103.3 all-gather.3
  360.5 261.4 all-reduce.6
where the time goes:
time: 632 us; the launch traced here: 630 us
  waiting for transfers between devices  532 us (84%)
  local copies, waits for them, and re-layouts  27.1 us (4%)
  matrix products  19.9 us (3%)
  between operations  14.6 us (2%)
  other arithmetic  13.5 us (2%)
  starting transfers between devices  13.3 us (2%)
  blocking collectives  9.37 us (1%)
    unnamed x5, waiting for transfers between devices  441 us
    all_gather x1, waiting for transfers between devices, body(): lax.all_gather(mixed_rows[None], ('sec', 'ep'), axis=0, tiled=True)  86.2 us
    another operation x3, local copies, waits for them, and re-layouts  19.4 us
    all_to_all x1, starting transfers between devices, body(): lax.all_to_all(incoming_state.astype(jnp.bfloat16), 'ep', split_axis=1, c...  13.2 us
  transfers between devices with their start and end apart: 4, of which 4 were waited for; matrix products, arithmetic and copies ran while one was open for 4% of the time, Pallas kernels for 0%

commit v1 on v0

v1 whole, which is shorter than its diff:
```python
import functools

import jax
import jax.numpy as jnp
from jax import lax
from jax.experimental import pallas as pl
from jax.experimental.pallas import tpu as pltpu
from jax.sharding import PartitionSpec as P

EPSILON = 1e-06
CORES = 2
CAPACITY = 32
MESH = pl.DeviceIdType.MESH
F32 = jnp.float32
BF16 = jnp.bfloat16
GRID = (4, 4, 8)


def iota(shape, dim):
    return lax.broadcasted_iota(jnp.int32, shape, dim)


def natural_row(position, grid):
    _, ny, nz = grid
    pair = 2 * CORES
    block = ny * pair
    zi = position // block
    yi = (position % block) // pair
    return yi * (nz * pair) + zi * pair + position % pair


def dot(a, b, dims=((1,), (0,)), precision=None):
    return lax.dot_general(a, b, (dims, ((), ())), preferred_element_type=F32, precision=precision)


def layer_kernel(
    grid,
    admit_ref,
    residual_ref,
    q_ref,
    k_ref,
    v_ref,
    arrived_ref,
    occupancy_ref,
    decay_ref,
    gain_ref,
    routes_ref,
    weight_ref,
    state_hbm,
    wo_hbm,
    gate_hbm,
    up_hbm,
    down_hbm,
    out_ref,
    state_v,
    wo_v,
    gate_v,
    up_v,
    down_v,
    heads_buf,
    partial,
    snd3,
    rcv3,
    own4,
    snd4,
    rcv4,
    snd5,
    rcv5,
    full,
    snd7,
    xin,
    snd8,
    rcv8,
    own9,
    snd9,
    rcv9,
    snd10,
    rcv10,
    local_sem,
    s2,
    r2,
    s3,
    r3,
    s4,
    r4,
    s5,
    r5,
    s6,
    r6,
    s7,
    r7,
    s8,
    r8,
    s9,
    r9,
    s10,
    r10,
):
    nx, ny, nz = grid
    slots = q_ref.shape[0]
    hd = q_ref.shape[1]
    rows = nx * slots
    rz = rows // nz
    cols = xin.shape[2]
    admitted = admit_ref.shape[0]

    x = lax.axis_index("sec")
    ep = lax.axis_index("ep")
    c = lax.rem(ep, CORES)
    z = lax.rem(ep // CORES, nz)
    y = ep // (CORES * nz)

    def at(xx, yy, zz, cc):
        return (xx, (yy * nz + zz) * CORES + cc)

    loads = [
        pltpu.make_async_copy(src, dst, local_sem.at[i])
        for i, (src, dst) in enumerate(
            (
                (state_hbm, state_v),
                (wo_hbm, wo_v),
                (gate_hbm, gate_v),
                (up_hbm, up_v),
                (down_hbm, down_v),
            )
        )
    ]
    for load in loads:
        load.start()

    barrier = pltpu.get_barrier_semaphore()
    partners = []
    for i in range(1, nx * ny):
        partners.append(at(lax.rem(x + i // ny, nx), lax.rem(y + i % ny, ny), z, c))
    for dz in range(1, nz):
        partners.append(at(x, y, lax.rem(z + dz, nz), c))
    for dy in range(ny):
        partners.append(at(x, lax.rem(y + dy, ny), z, 1 - c))
    for partner in partners:
        pl.semaphore_signal(barrier, inc=1, device_id=partner, device_id_type=MESH)

    q = q_ref[...].astype(F32)
    kk = k_ref[...].astype(F32)
    vv = v_ref[...].astype(F32)
    occupancy = occupancy_ref[...].astype(F32)
    eye = iota((slots, slots), 0) == iota((slots, slots), 1)
    kept = jnp.sum(jnp.where(eye, occupancy, 0.0), axis=1, keepdims=True)
    slot_row = iota((slots, 1), 0)
    taken = jnp.zeros((slots, 1), jnp.bool_)
    kb = hd // (ny * nz * CORES)
    wide = arrived_ref.shape[0]
    lane = iota((1, wide), 1)
    lane_request = (lane // kb) % admitted
    lane_slot = jnp.zeros((1, wide), jnp.int32)
    for a in range(admitted):
        slot = admit_ref[a] - x * slots
        taken = jnp.logical_or(taken, slot_row == slot)
        lane_slot = jnp.where(lane_request == a, slot, lane_slot)
    old_q = jnp.where(taken, 0.0, q * kept)
    lane2 = iota((hd, wide), 1)
    spread_key = (lane2 // (admitted * kb)) * kb + lane2 % kb
    repeat = (iota((hd, wide), 0) == spread_key).astype(BF16)
    new_q = dot(q.astype(BF16), repeat)
    new_q = jnp.where(slot_row == lane_slot, new_q, 0.0).astype(BF16)
    base_new = dot(new_q, arrived_ref[...])
    loads[0].wait()
    base_old = []
    row8 = iota((8, hd), 0)
    for chunk in range(slots // 8):
        part = old_q[chunk * 8 : chunk * 8 + 8]
        diagonal = jnp.concatenate(
            [jnp.where(row8 == s, part, 0.0) for s in range(8)], axis=1
        ).astype(BF16)
        states = state_v[chunk * 8 * hd : (chunk + 1) * 8 * hd, :].astype(BF16)
        base_old.append(dot(diagonal, states))
    base = jnp.concatenate(base_old, axis=0) + base_new
    raw = jnp.exp(-decay_ref[...]) * base + jnp.sum(q * kk, axis=1, keepdims=True) * vv
    power = jnp.mean(raw * raw, axis=1, keepdims=True)
    heads_buf[x] = (raw * lax.rsqrt(power + EPSILON)).astype(BF16)

    pl.semaphore_wait(barrier, len(partners))

    copies2 = []
    for dx in range(1, nx):
        copy = pltpu.make_async_remote_copy(
            heads_buf.at[x],
            heads_buf.at[x],
            s2.at[dx - 1],
            r2.at[dx - 1],
            device_id=at(lax.rem(x + dx, nx), y, z, c),
            device_id_type=MESH,
        )
        copy.start()
        copies2.append(copy)

    position0 = iota((rows, rows), 0)
    position1 = iota((rows, rows), 1)
    row_of0 = natural_row(position0, grid)
    row_of1 = natural_row(position1, grid)
    to_held = (position0 == row_of1).astype(F32)
    not_after = (row_of0 <= row_of1).astype(BF16)
    expert = iota((8, rows), 0) * (nz // 2) + z // 2
    hit = jnp.zeros((8, rows), jnp.bool_)
    weight = jnp.zeros((8, rows), F32)
    for t in range(routes_ref.shape[0]):
        route = jnp.broadcast_to(routes_ref[t : t + 1, :].astype(F32), (8, rows))
        route = dot(route.astype(BF16), to_held.astype(BF16))
        gate_value = jnp.broadcast_to(weight_ref[t : t + 1, :], (8, rows))
        gate_value = dot(gate_value, to_held, precision=lax.Precision.HIGHEST)
        same = route == expert.astype(F32)
        hit = jnp.logical_or(hit, same)
        weight = weight + jnp.where(same, gate_value, 0.0)
    rank = dot(hit.astype(F32).astype(BF16), not_after)
    rank = jnp.where(hit, rank, 0.0)
    place = (iota((CAPACITY, rows), 0) + 1).astype(F32)
    picks, slot_weights = [], []
    for yy in range(ny):
        chosen = rank[yy : yy + 1, :] == place
        picks.append(chosen.astype(F32))
        slot_weights.append(
            jnp.sum(jnp.where(chosen, weight[yy : yy + 1, :], 0.0), axis=1, keepdims=True)
        )
    pick = jnp.concatenate(picks, axis=0).astype(BF16)
    from_held = (position1 == row_of0).astype(BF16)

    loads[1].wait()
    for copy in copies2:
        copy.wait_recv()

    heads = heads_buf[...].reshape(rows, hd)
    heads = dot(from_held, heads).astype(BF16)
    first = z * rz + y * (2 * CORES) + c * 2
    group = pl.multiple_of((first // 8) * 8, 8)
    inside = first - group
    row_in_group = iota((8, cols), 0)
    for yy in range(ny):
        partial[yy] = dot(heads, wo_v[:, yy * cols : (yy + 1) * cols])
        res = residual_ref[:, yy * cols : (yy + 1) * cols].astype(F32)
        add = jnp.where(row_in_group == inside, res[0:1, :], 0.0) + jnp.where(
            row_in_group == inside + 1, res[1:2, :], 0.0
        )
        partial[yy, pl.ds(group, 8), :] += add
        snd3[yy] = partial[yy].astype(BF16)
    copies3 = []
    for dy in range(1, ny):
        to = lax.rem(y + dy, ny)
        copy = pltpu.make_async_remote_copy(
            snd3.at[to],
            rcv3.at[dy - 1],
            s3.at[dy - 1],
            r3.at[dy - 1],
            device_id=at(x, to, z, c),
            device_id_type=MESH,
        )
        copy.start()
        copies3.append(copy)
    total = partial[y]
    for i, copy in enumerate(copies3):
        copy.wait_recv()
        total = total + rcv3[i].astype(F32)

    for zz in range(nz):
        own4[zz] = total[zz * rz : (zz + 1) * rz]
        snd4[zz] = total[zz * rz : (zz + 1) * rz].astype(BF16)
    copies4 = []
    for dz in range(1, nz):
        to = lax.rem(z + dz, nz)
        copy = pltpu.make_async_remote_copy(
            snd4.at[to],
            rcv4.at[dz - 1],
            s4.at[dz - 1],
            r4.at[dz - 1],
            device_id=at(x, y, to, c),
            device_id_type=MESH,
        )
        copy.start()
        copies4.append(copy)
    mine = own4[z]
    for i, copy in enumerate(copies4):
        copy.wait_recv()
        mine = mine + rcv4[i].astype(F32)

    snd5[...] = mine
    copy5 = pltpu.make_async_remote_copy(
        snd5, rcv5, s5.at[0], r5.at[0], device_id=at(x, y, z, 1 - c), device_id_type=MESH
    )
    copy5.start()
    copy5.wait_recv()
    mixed = (mine + rcv5[...]).astype(BF16)
    full[z] = mixed

    copies6 = []
    for dz in range(1, nz):
        copy = pltpu.make_async_remote_copy(
            full.at[z],
            full.at[z],
            s6.at[dz - 1],
            r6.at[dz - 1],
            device_id=at(x, y, lax.rem(z + dz, nz), c),
            device_id_type=MESH,
        )
        copy.start()
        copies6.append(copy)
    for copy in copies6:
        copy.wait_recv()

    here = x * ny + y
    picked = dot(pick, full[...].reshape(rows, cols)).astype(BF16)
    for yy in range(ny):
        snd7[yy] = picked[yy * CAPACITY : (yy + 1) * CAPACITY]

    def to_experts(i):
        xx, yy = lax.rem(x + i // ny, nx), lax.rem(y + lax.rem(i, ny), ny)
        return pltpu.make_async_remote_copy(
            snd7.at[yy],
            xin.at[here],
            s7.at[i],
            r7.at[i],
            device_id=at(xx, yy, z, c),
            device_id_type=MESH,
        )

    @pl.loop(1, nx * ny)
    def _(i):
        to_experts(i).start()

    xin[here] = snd7[y]
    for load in loads[2:]:
        load.wait()

    def one_block(block, carry):
        gate_sum, up_sum, squares = carry
        taken_rows = xin[block].astype(F32)
        columns = pl.ds(pl.multiple_of(block * cols, cols), cols)
        squares = squares + jnp.sum(taken_rows * taken_rows, axis=1, keepdims=True)
        scaled = (taken_rows * gain_ref[:, columns]).astype(BF16)
        gate_sum = gate_sum + dot(scaled, gate_v[:, columns], ((1,), (1,)))
        up_sum = up_sum + dot(scaled, up_v[:, columns], ((1,), (1,)))
        return gate_sum, up_sum, squares

    def arriving(i, carry):
        to_experts(i).wait_recv()
        xx = lax.rem(x - i // ny + nx, nx)
        yy = lax.rem(y - lax.rem(i, ny) + ny, ny)
        return one_block(xx * ny + yy, carry)

    hidden_units = gate_v.shape[0]
    carry = (
        jnp.zeros((CAPACITY, hidden_units), F32),
        jnp.zeros((CAPACITY, hidden_units), F32),
        jnp.zeros((CAPACITY, 1), F32),
    )
    carry = one_block(here, carry)
    gate_sum, up_sum, squares = lax.fori_loop(1, nx * ny, arriving, carry)
    scale = lax.rsqrt(squares / (nx * ny * cols) + EPSILON)
    gate_sum = gate_sum * scale
    up_sum = up_sum * scale
    hidden = (gate_sum / (1.0 + jnp.exp(-gate_sum)) * up_sum).astype(BF16)

    def back(i):
        xx, yy = lax.rem(x + i // ny, nx), lax.rem(y + lax.rem(i, ny), ny)
        return pltpu.make_async_remote_copy(
            snd8.at[i],
            rcv8.at[here],
            s8.at[i],
            r8.at[i],
            device_id=at(xx, yy, z, c),
            device_id_type=MESH,
        )

    def down_block(block):
        columns = pl.ds(pl.multiple_of(block * cols, cols), cols)
        return dot(hidden, down_v[:, columns]).astype(BF16)

    @pl.loop(1, nx * ny)
    def _(i):
        xx, yy = lax.rem(x + i // ny, nx), lax.rem(y + lax.rem(i, ny), ny)
        snd8[i] = down_block(xx * ny + yy)
        back(i).start()

    rcv8[here] = down_block(here)

    @pl.loop(1, nx * ny)
    def _(i):
        back(i).wait_recv()

    summed = []
    for yy in range(ny):
        term = rcv8[yy].astype(F32)
        for xx in range(1, nx):
            term = term + rcv8[xx * ny + yy].astype(F32)
        summed.append(term * slot_weights[yy])
    summed = jnp.concatenate(summed, axis=0).astype(BF16)
    routed = dot(pick, summed, ((0,), (0,)))
    for zz in range(nz):
        own9[zz] = routed[zz * rz : (zz + 1) * rz]
        snd9[zz] = routed[zz * rz : (zz + 1) * rz].astype(BF16)
    copies9 = []
    for dz in range(1, nz):
        to = lax.rem(z + dz, nz)
        copy = pltpu.make_async_remote_copy(
            snd9.at[to],
            rcv9.at[dz - 1],
            s9.at[dz - 1],
            r9.at[dz - 1],
            device_id=at(x, y, to, c),
            device_id_type=MESH,
        )
        copy.start()
        copies9.append(copy)
    block = own9[z] + mixed.astype(F32) * jnp.where(c == 0, 1.0, 0.0)
    for i, copy in enumerate(copies9):
        copy.wait_recv()
        block = block + rcv9[i].astype(F32)

    for i in range(ny * CORES):
        snd10[i] = block[2 * i : 2 * i + 2, :]
    spot = y * CORES + c
    copies10 = []
    for i in range(1, ny * CORES):
        to_y, to_c = lax.rem(y + i // CORES, ny), lax.rem(c + i % CORES, CORES)
        copy = pltpu.make_async_remote_copy(
            snd10.at[to_y * CORES + to_c],
            rcv10.at[spot],
            s10.at[i - 1],
            r10.at[i - 1],
            device_id=at(x, to_y, z, to_c),
            device_id_type=MESH,
        )
        copy.start()
        copies10.append(copy)
    rcv10[spot] = snd10[spot]
    for copy in copies10:
        copy.wait_recv()
    for yy in range(ny):
        out_ref[:, yy * cols : (yy + 1) * cols] = (
            rcv10[yy * CORES] + rcv10[yy * CORES + 1]
        ).astype(BF16)

    for copy in copies2 + copies3 + copies4 + [copy5] + copies6 + copies9 + copies10:
        copy.wait_send()

    @pl.loop(1, nx * ny)
    def _(i):
        to_experts(i).wait_send()
        back(i).wait_send()


def body(
    grid,
    residual_in,
    queries,
    keys_new,
    values_new,
    cached_state,
    incoming_state,
    admit_slot,
    occupancy,
    decay_rate,
    out_proj,
    norm_gain,
    routes,
    route_weight,
    gate_proj,
    up_proj,
    down_proj,
):
    nx, ny, nz = grid
    slots, hd = queries.shape
    rows = nx * slots
    rz = rows // nz
    cols = residual_in.shape[1] // ny
    blocks = nx * ny
    units = gate_proj.shape[2]
    width = gate_proj.shape[1]
    admitted, heads, kb, _ = incoming_state.shape

    arrived = lax.all_to_all(
        incoming_state.astype(BF16).transpose(1, 0, 2, 3).reshape(heads, admitted * kb, hd),
        "ep",
        split_axis=0,
        concat_axis=0,
        tiled=True,
    ).reshape(heads * admitted * kb, hd)

    vmem = pl.BlockSpec(memory_space=pltpu.VMEM)
    anywhere = pl.BlockSpec(memory_space=pl.ANY)
    dma = lambda n: pltpu.SemaphoreType.DMA((n,))
    scratch = [
        pltpu.VMEM((slots * hd, hd), F32),
        pltpu.VMEM(out_proj.shape, BF16),
        pltpu.VMEM((units, width), BF16),
        pltpu.VMEM((units, width), BF16),
        pltpu.VMEM((units, width), BF16),
        pltpu.VMEM((nx, slots, hd), BF16),
        pltpu.VMEM((ny, rows, cols), F32),
        pltpu.VMEM((ny, rows, cols), BF16),
        pltpu.VMEM((ny - 1, rows, cols), BF16),
        pltpu.VMEM((nz, rz, cols), F32),
        pltpu.VMEM((nz, rz, cols), BF16),
        pltpu.VMEM((nz - 1, rz, cols), BF16),
        pltpu.VMEM((rz, cols), F32),
        pltpu.VMEM((rz, cols), F32),
        pltpu.VMEM((nz, rz, cols), BF16),
        pltpu.VMEM((ny, CAPACITY, cols), BF16),
        pltpu.VMEM((blocks, CAPACITY, cols), BF16),
        pltpu.VMEM((blocks, CAPACITY, cols), BF16),
        pltpu.VMEM((blocks, CAPACITY, cols), BF16),
        pltpu.VMEM((nz, rz, cols), F32),
        pltpu.VMEM((nz, rz, cols), BF16),
        pltpu.VMEM((nz - 1, rz, cols), BF16),
        pltpu.VMEM((ny * CORES, 2, cols), F32),
        pltpu.VMEM((ny * CORES, 2, cols), F32),
        dma(5),
    ]
    for n in (nx - 1, ny - 1, nz - 1, 1, nz - 1, blocks, blocks, nz - 1, ny * CORES - 1):
        scratch += [dma(n), dma(n)]

    return pl.pallas_call(
        functools.partial(layer_kernel, grid),
        out_shape=jax.ShapeDtypeStruct(residual_in.shape, BF16),
        in_specs=[pl.BlockSpec(memory_space=pltpu.SMEM)] + [vmem] * 10 + [anywhere] * 5,
        out_specs=vmem,
        scratch_shapes=scratch,
        compiler_params=pltpu.CompilerParams(
            collective_id=0, has_side_effects=True, vmem_limit_bytes=48 * 2**20
        ),
    )(
        admit_slot,
        residual_in,
        queries,
        keys_new,
        values_new,
        arrived,
        occupancy.reshape(1, slots),
        decay_rate.reshape(1, 1),
        norm_gain.reshape(1, width),
        routes.T,
        route_weight.T,
        cached_state.reshape(slots * hd, hd),
        out_proj,
        gate_proj[0].T,
        up_proj[0].T,
        down_proj[0],
    )


def solution(mesh):
    in_specs = (
        P("ep", "sec"),
        P("sec", "ep"),
        P("sec", "ep"),
        P("sec", "ep"),
        P("sec", "ep", None, None),
        P("sec", None, "ep", None),
        P("sec"),
        P("sec"),
        P("ep"),
        P("ep", "sec"),
        P(),
        P(),
        P(),
        P("ep", None, "sec"),
        P("ep", None, "sec"),
        P("ep", "sec", None),
    )
    return jax.shard_map(
        functools.partial(body, GRID),
        mesh=mesh,
        in_specs=in_specs,
        out_specs=P("ep", "sec"),
        check_vma=False,
    )
```

time: 632 us -> 89.2 us (0.14)
  waiting for transfers between devices: 532 us -> 9.72 us
  Pallas kernels: 0 us -> 54.1 us
  matrix products: 19.9 us -> 0 us
  local copies, waits for them, and re-layouts: 27.1 us -> 11.1 us
  between operations: 14.6 us -> 0.68 us
  other arithmetic: 13.5 us -> 0 us
  blocking collectives: 9.37 us -> 0 us
    unnamed x5 -> x0, waiting for transfers between devices: 441 us -> none
    all_gather x1 -> x0, waiting for transfers between devices: 86.2 us -> none  [body(): lax.all_gather(mixed_rows[None], ('sec', 'ep'), axis=0, tiled=True)]
    pallas_call x0 -> x1, Pallas kernels: none -> 54.1 us  [body(): pl.pallas_call(functools.partial(layer_kernel, grid), out_shape=jax.Shape...]
    dot_general x9 -> x0, matrix products: 19.9 us -> none  [the longest x1 5.82 us: body(): jnp.einsum('pkf,pfsc->pskc', hidden, down_split, preferred_element_type=j...]
    another operation x3 -> x0, local copies, waits for them, and re-layouts: 19.4 us -> none
    all_gather x1 -> x0, blocking collectives: 9.37 us -> none  [body(): all_heads = lax.all_gather(head_out, 'sec', axis=0, tiled=True)]
    convert_element_type x6 -> x0, other arithmetic: 8.49 us -> none  [the longest x1 4.94 us: body(): (whole_rows * lax.rsqrt(row_power + epsilon)[None, :, None] * gain_rows)....]
    unnamed x20 -> x24, local copies, waits for them, and re-layouts: 2.45 us -> 10.3 us
  transfers between devices with their start and end apart: 4 -> 1, of which waited for: 4 -> 1; matrix products, arithmetic and copies ran while one was open for 4% -> 0% of each run, Pallas kernels for 0% -> 0%
where the time goes in v1:
time: 89.2 us; the launch traced here: 88.7 us
  Pallas kernels  54.1 us (61%)
  starting transfers between devices  13.2 us (15%)
  local copies, waits for them, and re-layouts  11.1 us (12%)
  waiting for transfers between devices  9.72 us (11%)
    pallas_call x1, Pallas kernels, body(): pl.pallas_call(functools.partial(layer_kernel, grid), out_shape=jax.Shape...  54.1 us
    all_to_all x1, starting transfers between devices, body(): lax.all_to_all(incoming_state.astype(BF16).transpose(1, 0, 2, 3).reshape(...  13.2 us
    unnamed x24, local copies, waits for them, and re-layouts  10.3 us
    all_to_all x1, waiting for transfers between devices, body(): lax.all_to_all(incoming_state.astype(BF16).transpose(1, 0, 2, 3).reshape(...  9.72 us
  transfers between devices with their start and end apart: 1, of which 1 were waited for; matrix products, arithmetic and copies ran while one was open for 0% of the time, Pallas kernels for 0%

profile of v1, /device:TPU:1, one launch (start us, length us, event | category | flops | bytes accessed | tf_op | source)
XLA Modules:
  0.0 88.7 jit_solution(4319973229313745591)
XLA Ops:
  0.0 1.0 %copy.22 = bf16[4,64,2,128]{3,1,2,0:T(8,128)(2,1)S(1)} copy(f32[4,64,2,128]{3,2,1,0:T(2,128)} %param.21) | data formatting | bytes 393216 | tf_op args[5]
  1.0 0.7 copy.20
  1.7 13.2 %all-to-all-start = ((bf16[64,8,128]{2,1,0:T(8,128)(2,1)}), bf16[64,8,128]{2,1,0:T(8,128)(2,1)S(1)}, u32[]{:S(2)}, u32[]{:S(2)}) async-start(bf16[64,8,128]{2,1,0:T(8,128)(2,1)} %copy.20), calls=%async_computation | async-start | bytes 262144 | tf_op jit(solution)/shard_map/all_to_all | solution.py:478
  15.5 9.7 %all-to-all-done = bf16[64,8,128]{2,1,0:T(8,128)(2,1)S(1)} async-done(((bf16[64,8,128]{2,1,0:T(8,128)(2,1)}), bf16[64,8,128]{2,1,0:T(8,128)(2,1)S(1)}, u32[]{:S(2)}, u32[]{:S(2)}) %all-to-all-start) | async-done | bytes 131104 | tf_op jit(solution)/shard_map/all_to_all | solution.py:478
  25.2 0.0 copy-start
  25.2 1.6 %copy-done = f32[32,1,128,128]{3,2,1,0:T(8,128)S(1)} copy-done((f32[32,1,128,128]{3,2,1,0:T(8,128)S(1)}, f32[32,1,128,128]{3,2,1,0:T(8,128)}, u32[]{:S(2)}) %copy-start) | copy-done | bytes 2097176
  26.8 0.0 copy-start.1
  26.8 1.0 %copy-done.1 = bf16[128,1536]{1,0:T(8,128)(2,1)S(1)} copy-done((bf16[128,1536]{1,0:T(8,128)(2,1)S(1)}, bf16[128,1536]{1,0:T(8,128)(2,1)}, u32[]{:S(2)}) %copy-start.1) | copy-done | bytes 393240
  27.8 0.0 copy-start.2
  27.8 0.7 copy-done.2
  28.6 0.0 copy-start.3
  28.6 0.7 copy-done.3
  29.3 0.0 copy-start.4
  29.3 0.7 copy-done.4
  30.0 0.0 copy-start.5
  30.0 0.7 copy-done.5
  30.7 0.0 copy-start.6
  30.7 0.7 copy-done.6
  31.4 0.0 copy-start.7
  31.4 0.7 copy-done.7
  32.0 0.0 copy-start.8
  32.0 0.7 copy-done.8
  32.7 0.0 copy-start.9
  32.7 0.7 copy-done.9
  33.4 0.0 copy-start.10
  33.4 0.7 copy-done.10
  34.0 54.1 %shard_map.154 = bf16[2,1536]{1,0:T(2,128)(2,1)S(1)} custom-call(s32[4]{0:T(128)S(1)} %copy-done.9, bf16[2,1536]{1,0:T(2,128)(2,1)S(1)} %copy-done.6, bf16[32,128]{1,0:T(8,128)(2,1)S(1)} %copy-done.3, bf16[32,128]{1,0:T(8,128)(2,1)S(1)} %copy-done.4, bf16[32,128]{1,0:T(8,128)(2,1)S(1)} %copy-done.5, bf16[512,128]{1,0:T(8,128)(2,1)S(1)} %bitcast.19, ...), custom_call_target="tpu_custom_call" | custom-call | tf_op jit(solution)/shard_map/pallas_call | solution.py:519
  88.1 0.6 copy.25
Async XLA Ops:
  1.7 23.5 %all-to-all-start = ((bf16[64,8,128]{2,1,0:T(8,128)(2,1)}), bf16[64,8,128]{2,1,0:T(8,128)(2,1)S(1)}, u32[]{:S(2)}, u32[]{:S(2)}) async-start(bf16[64,8,128]{2,1,0:T(8,128)(2,1)} %copy.20), calls=%async_computation | async-start | bytes 262144 | tf_op jit(solution)/shard_map/all_to_all | solution.py:478
  25.2 1.6 %copy-start = (f32[32,1,128,128]{3,2,1,0:T(8,128)S(1)}, f32[32,1,128,128]{3,2,1,0:T(8,128)}, u32[]{:S(2)}) copy-start(f32[32,1,128,128]{3,2,1,0:T(8,128)} %param.20) | copy-start | bytes 6291460
  26.8 1.0 %copy-start.1 = (bf16[128,1536]{1,0:T(8,128)(2,1)S(1)}, bf16[128,1536]{1,0:T(8,128)(2,1)}, u32[]{:S(2)}) copy-start(bf16[128,1536]{1,0:T(8,128)(2,1)} %wo_hbm.1) | copy-start | bytes 1179652
  27.8 0.7 copy-start.2
  28.6 0.7 copy-start.3
  29.3 0.7 copy-start.4
  30.0 0.7 copy-start.5
  30.7 0.7 copy-start.6
  31.4 0.7 copy-start.7
  32.0 0.7 copy-start.8
  32.7 0.7 copy-start.9
  33.4 0.7 copy-start.10

commit v2 on v1

--- a/solution.py
+++ b/solution.py
@@ -10,6 +10,7 @@
 EPSILON = 1e-06
 CORES = 2
 CAPACITY = 32
+VMEM_BYTES = 62 * 2**20
 MESH = pl.DeviceIdType.MESH
 F32 = jnp.float32
 BF16 = jnp.bfloat16
@@ -35,28 +36,26 @@
 
 def layer_kernel(
     grid,
+    operands,
+    out_ref,
+    incoming_v,
     admit_ref,
-    residual_ref,
+    occupancy_ref,
     q_ref,
     k_ref,
     v_ref,
-    arrived_ref,
-    occupancy_ref,
     decay_ref,
-    gain_ref,
     routes_ref,
     weight_ref,
-    state_hbm,
-    wo_hbm,
-    gate_hbm,
-    up_hbm,
-    down_hbm,
-    out_ref,
+    residual_ref,
+    gain_ref,
     state_v,
     wo_v,
     gate_v,
     up_v,
     down_v,
+    snd1,
+    rcv1,
     heads_buf,
     partial,
     snd3,
@@ -77,6 +76,8 @@
     snd10,
     rcv10,
     local_sem,
+    s1,
+    r1,
     s2,
     r2,
     s3,
@@ -97,12 +98,14 @@
     r10,
 ):
     nx, ny, nz = grid
-    slots = q_ref.shape[0]
-    hd = q_ref.shape[1]
+    slots, hd = q_ref.shape
+    parts = ny * nz * CORES
+    kb = hd // parts
     rows = nx * slots
     rz = rows // nz
     cols = xin.shape[2]
     admitted = admit_ref.shape[0]
+    wide = parts * admitted * kb
 
     x = lax.axis_index("sec")
     ep = lax.axis_index("ep")
@@ -113,31 +116,79 @@
     def at(xx, yy, zz, cc):
         return (xx, (yy * nz + zz) * CORES + cc)
 
+    incoming_hbm, *others = operands
+    held = (
+        admit_ref,
+        occupancy_ref,
+        q_ref,
+        k_ref,
+        v_ref,
+        decay_ref,
+        state_v,
+        routes_ref,
+        weight_ref,
+        residual_ref,
+        wo_v,
+        gain_ref,
+        gate_v,
+        up_v,
+        down_v,
+    )
+    incoming_loads = [
+        pltpu.make_async_copy(
+            incoming_hbm.at[a], incoming_v.at[:, kb * a : kb * (a + 1), :], local_sem.at[a]
+        )
+        for a in range(admitted)
+    ]
     loads = [
-        pltpu.make_async_copy(src, dst, local_sem.at[i])
-        for i, (src, dst) in enumerate(
-            (
-                (state_hbm, state_v),
-                (wo_hbm, wo_v),
-                (gate_hbm, gate_v),
-                (up_hbm, up_v),
-                (down_hbm, down_v),
-            )
-        )
+        pltpu.make_async_copy(src, dst, local_sem.at[admitted + i])
+        for i, (src, dst) in enumerate(zip(others, held))
     ]
-    for load in loads:
+    for load in incoming_loads + loads:
         load.start()
 
     barrier = pltpu.get_barrier_semaphore()
-    partners = []
-    for i in range(1, nx * ny):
-        partners.append(at(lax.rem(x + i // ny, nx), lax.rem(y + i % ny, ny), z, c))
-    for dz in range(1, nz):
-        partners.append(at(x, y, lax.rem(z + dz, nz), c))
-    for dy in range(ny):
-        partners.append(at(x, lax.rem(y + dy, ny), z, 1 - c))
-    for partner in partners:
+
+    @pl.loop(1, parts)
+    def _(i):
+        pl.semaphore_signal(
+            barrier, inc=1, device_id=(x, lax.rem(ep + i, parts)), device_id_type=MESH
+        )
+
+    @pl.loop(ny, nx * ny)
+    def _(i):
+        partner = at(lax.rem(x + i // ny, nx), lax.rem(y + lax.rem(i, ny), ny), z, c)
         pl.semaphore_signal(barrier, inc=1, device_id=partner, device_id_type=MESH)
+
+    for load in incoming_loads:
+        load.wait()
+    snd1[...] = incoming_v[...].astype(BF16)
+    pl.semaphore_wait(barrier, parts - 1 + (nx - 1) * ny)
+
+    @pl.loop(1, parts)
+    def _(i):
+        to = lax.rem(ep + i, parts)
+        pltpu.make_async_remote_copy(
+            snd1.at[to],
+            rcv1.at[ep],
+            s1.at[0],
+            r1.at[0],
+            device_id=(x, to),
+            device_id_type=MESH,
+        ).start()
+
+    rcv1[ep] = snd1[ep]
+    every1 = pltpu.make_async_remote_copy(
+        snd1.at[pl.ds(0, parts - 1)],
+        rcv1.at[pl.ds(0, parts - 1)],
+        s1.at[0],
+        r1.at[0],
+        device_id=(x, lax.rem(ep + 1, parts)),
+        device_id_type=MESH,
+    )
+
+    for load in loads[:7]:
+        load.wait()
 
     q = q_ref[...].astype(F32)
     kk = k_ref[...].astype(F32)
@@ -147,8 +198,6 @@
     kept = jnp.sum(jnp.where(eye, occupancy, 0.0), axis=1, keepdims=True)
     slot_row = iota((slots, 1), 0)
     taken = jnp.zeros((slots, 1), jnp.bool_)
-    kb = hd // (ny * nz * CORES)
-    wide = arrived_ref.shape[0]
     lane = iota((1, wide), 1)
     lane_request = (lane // kb) % admitted
     lane_slot = jnp.zeros((1, wide), jnp.int32)
@@ -162,8 +211,6 @@
     repeat = (iota((hd, wide), 0) == spread_key).astype(BF16)
     new_q = dot(q.astype(BF16), repeat)
     new_q = jnp.where(slot_row == lane_slot, new_q, 0.0).astype(BF16)
-    base_new = dot(new_q, arrived_ref[...])
-    loads[0].wait()
     base_old = []
     row8 = iota((8, hd), 0)
     for chunk in range(slots // 8):
@@ -173,12 +220,12 @@
         ).astype(BF16)
         states = state_v[chunk * 8 * hd : (chunk + 1) * 8 * hd, :].astype(BF16)
         base_old.append(dot(diagonal, states))
-    base = jnp.concatenate(base_old, axis=0) + base_new
+    every1.wait_recv()
+    arrived = rcv1[...].astype(F32).reshape(wide, hd).astype(BF16)
+    base = jnp.concatenate(base_old, axis=0) + dot(new_q, arrived)
     raw = jnp.exp(-decay_ref[...]) * base + jnp.sum(q * kk, axis=1, keepdims=True) * vv
     power = jnp.mean(raw * raw, axis=1, keepdims=True)
     heads_buf[x] = (raw * lax.rsqrt(power + EPSILON)).astype(BF16)
-
-    pl.semaphore_wait(barrier, len(partners))
 
     copies2 = []
     for dx in range(1, nx):
@@ -192,6 +239,9 @@
         )
         copy.start()
         copies2.append(copy)
+
+    for load in loads[7:9]:
+        load.wait()
 
     position0 = iota((rows, rows), 0)
     position1 = iota((rows, rows), 1)
@@ -223,7 +273,8 @@
     pick = jnp.concatenate(picks, axis=0).astype(BF16)
     from_held = (position1 == row_of0).astype(BF16)
 
-    loads[1].wait()
+    for load in loads[9:12]:
+        load.wait()
     for copy in copies2:
         copy.wait_recv()
 
@@ -325,7 +376,7 @@
         to_experts(i).start()
 
     xin[here] = snd7[y]
-    for load in loads[2:]:
+    for load in loads[12:]:
         load.wait()
 
     def one_block(block, carry):
@@ -437,6 +488,7 @@
             rcv10[yy * CORES] + rcv10[yy * CORES + 1]
         ).astype(BF16)
 
+    every1.wait_send()
     for copy in copies2 + copies3 + copies4 + [copy5] + copies6 + copies9 + copies10:
         copy.wait_send()
 
@@ -473,25 +525,30 @@
     blocks = nx * ny
     units = gate_proj.shape[2]
     width = gate_proj.shape[1]
-    admitted, heads, kb, _ = incoming_state.shape
-
-    arrived = lax.all_to_all(
-        incoming_state.astype(BF16).transpose(1, 0, 2, 3).reshape(heads, admitted * kb, hd),
-        "ep",
-        split_axis=0,
-        concat_axis=0,
-        tiled=True,
-    ).reshape(heads * admitted * kb, hd)
+    admitted, parts, kb, _ = incoming_state.shape
 
     vmem = pl.BlockSpec(memory_space=pltpu.VMEM)
     anywhere = pl.BlockSpec(memory_space=pl.ANY)
     dma = lambda n: pltpu.SemaphoreType.DMA((n,))
     scratch = [
+        pltpu.VMEM((parts, admitted * kb, hd), F32),
+        pltpu.SMEM(admit_slot.shape, jnp.int32),
+        pltpu.VMEM((1, slots), jnp.int32),
+        pltpu.VMEM((slots, hd), BF16),
+        pltpu.VMEM((slots, hd), BF16),
+        pltpu.VMEM((slots, hd), BF16),
+        pltpu.VMEM((1, 1), F32),
+        pltpu.VMEM((routes.shape[1], rows), jnp.int32),
+        pltpu.VMEM((routes.shape[1], rows), F32),
+        pltpu.VMEM(residual_in.shape, BF16),
+        pltpu.VMEM((1, width), F32),
         pltpu.VMEM((slots * hd, hd), F32),
         pltpu.VMEM(out_proj.shape, BF16),
         pltpu.VMEM((units, width), BF16),
         pltpu.VMEM((units, width), BF16),
         pltpu.VMEM((units, width), BF16),
+        pltpu.VMEM((parts, admitted * kb, hd), BF16),
+        pltpu.VMEM((parts, admitted * kb, hd), BF16),
         pltpu.VMEM((nx, slots, hd), BF16),
         pltpu.VMEM((ny, rows, cols), F32),
         pltpu.VMEM((ny, rows, cols), BF16),
@@ -511,34 +568,37 @@
         pltpu.VMEM((nz - 1, rz, cols), BF16),
         pltpu.VMEM((ny * CORES, 2, cols), F32),
         pltpu.VMEM((ny * CORES, 2, cols), F32),
-        dma(5),
+        dma(admitted + 15),
     ]
-    for n in (nx - 1, ny - 1, nz - 1, 1, nz - 1, blocks, blocks, nz - 1, ny * CORES - 1):
+    for n in (1, nx - 1, ny - 1, nz - 1, 1, nz - 1, blocks, blocks, nz - 1, ny * CORES - 1):
         scratch += [dma(n), dma(n)]
 
+    def kernel(*refs):
+        layer_kernel(grid, refs[:16], *refs[16:])
+
     return pl.pallas_call(
-        functools.partial(layer_kernel, grid),
+        kernel,
         out_shape=jax.ShapeDtypeStruct(residual_in.shape, BF16),
-        in_specs=[pl.BlockSpec(memory_space=pltpu.SMEM)] + [vmem] * 10 + [anywhere] * 5,
+        in_specs=[anywhere] * 16,
         out_specs=vmem,
         scratch_shapes=scratch,
         compiler_params=pltpu.CompilerParams(
-            collective_id=0, has_side_effects=True, vmem_limit_bytes=48 * 2**20
+            collective_id=0, has_side_effects=True, vmem_limit_bytes=VMEM_BYTES
         ),
     )(
+        incoming_state,
         admit_slot,
-        residual_in,
+        occupancy.reshape(1, slots),
         queries,
         keys_new,
         values_new,
-        arrived,
-        occupancy.reshape(1, slots),
         decay_rate.reshape(1, 1),
-        norm_gain.reshape(1, width),
+        cached_state.reshape(slots * hd, hd),
         routes.T,
         route_weight.T,
-        cached_state.reshape(slots * hd, hd),
+        residual_in,
         out_proj,
+        norm_gain.reshape(1, width),
         gate_proj[0].T,
         up_proj[0].T,
         down_proj[0],

time: 89.2 us -> 73.8 us (0.83)
  Pallas kernels: 54.1 us -> 71.7 us
  starting transfers between devices: 13.2 us -> 0 us
  local copies, waits for them, and re-layouts: 11.1 us -> 1.29 us
  waiting for transfers between devices: 9.72 us -> 0 us
    pallas_call x1, Pallas kernels: 54.1 us -> 71.7 us  [body(): pl.pallas_call(kernel, out_shape=jax.ShapeDtypeStruct(residual_in.shape,...]
    all_to_all x1 -> x0, starting transfers between devices: 13.2 us -> none  [body(): lax.all_to_all(incoming_state.astype(BF16).transpose(1, 0, 2, 3).reshape(...]
    all_to_all x1 -> x0, waiting for transfers between devices: 9.72 us -> none  [body(): lax.all_to_all(incoming_state.astype(BF16).transpose(1, 0, 2, 3).reshape(...]
    unnamed x24 -> x1, local copies, waits for them, and re-layouts: 10.3 us -> 1.29 us
  transfers between devices with their start and end apart: 1 -> 0, of which waited for: 1 -> 0; matrix products, arithmetic and copies ran while one was open for 0% -> 0% of each run, Pallas kernels for 0% -> 0%
where the time goes in v2:
time: 73.8 us; the launch traced here: 73.7 us
  Pallas kernels  71.7 us (97%)
  local copies, waits for them, and re-layouts  1.29 us (2%)
    pallas_call x1, Pallas kernels, body(): pl.pallas_call(kernel, out_shape=jax.ShapeDtypeStruct(residual_in.shape,...  71.7 us

profile of v2, /device:TPU:1, one launch (start us, length us, event | category | flops | bytes accessed | tf_op | source)
XLA Modules:
  0.0 73.7 jit_solution(14860568211620735521)
XLA Ops:
  0.7 71.7 %shard_map.154 = bf16[2,1536]{1,0:T(2,128)(2,1)} custom-call(f32[4,64,2,128]{3,2,1,0:T(2,128)} %refs_0_.1, s32[4]{0:T(128)} %refs_1_.1, s32[1,32]{1,0:T(1,128)} %bitcast.21, bf16[32,128]{1,0:T(8,128)(2,1)} %refs_3_.1, bf16[32,128]{1,0:T(8,128)(2,1)} %refs_4_.1, bf16[32,128]{1,0:T(8,128)(2,1)} %refs_5_.1, f32[1,1]{1,0:T(1,128)} %bitcast.13.refs_6_, ...), custom_call_target="tpu_custom_call" | custom-call | tf_op jit(solution)/shard_map/pallas_call | solution.py:579
  72.4 1.3 %copy.19 = bf16[2,1536]{1,0:T(2,128)(2,1)} copy(bf16[2,1536]{1,0:T(2,128)(2,1)} %shard_map.154) | data formatting | bytes 12288

commit v3 on v2

v3 whole, which is shorter than its diff:
```python
import functools

import jax
import jax.numpy as jnp
from jax import lax
from jax.experimental import pallas as pl
from jax.experimental.pallas import tpu as pltpu
from jax.sharding import PartitionSpec as P

EPSILON = 1e-06
CORES = 2
CAPACITY = 32
VMEM_BYTES = 62 * 2**20
MESH = pl.DeviceIdType.MESH
F32 = jnp.float32
BF16 = jnp.bfloat16
GRID = (4, 4, 8)


def iota(shape, dim):
    return lax.broadcasted_iota(jnp.int32, shape, dim)


def natural_row(position, grid):
    _, ny, nz = grid
    half = 2 * ny
    zi = position // (CORES * half)
    ci = (position // half) % CORES
    yi = (position % half) // 2
    return (yi * nz + zi) * (2 * CORES) + ci * 2 + position % 2


def far_first(*sizes):
    steps = [()]
    for size in sizes:
        steps = [step + (i,) for step in steps for i in range(size)]

    def distance(step):
        return sum(min(i, size - i) for i, size in zip(step, sizes))

    return sorted(steps, key=lambda step: -distance(step))[:-1]


def dot(a, b, dims=((1,), (0,)), precision=None):
    return lax.dot_general(a, b, (dims, ((), ())), preferred_element_type=F32, precision=precision)


def layer_kernel(
    grid,
    operands,
    out_ref,
    incoming_v,
    admit_ref,
    occupancy_ref,
    q_ref,
    k_ref,
    v_ref,
    decay_ref,
    routes_ref,
    weight_ref,
    residual_ref,
    gain_ref,
    state_v,
    wo_v,
    gate_v,
    up_v,
    down_v,
    snd1,
    pair1,
    rcv1,
    heads_buf,
    partial,
    snd3,
    rcv3,
    snd4,
    rcv4,
    full,
    snd7,
    xin,
    snd8,
    rcv8,
    own9,
    snd9,
    rcv9,
    snd10,
    rcv10,
    local_sem,
    s0,
    r0,
    s1,
    r1,
    s2,
    r2,
    s3,
    r3,
    s4,
    r4,
    s5,
    r5,
    s6,
    r6,
    s7,
    r7,
    s8,
    r8,
    s9,
    r9,
    s10,
    r10,
):
    nx, ny, nz = grid
    slots, hd = q_ref.shape
    parts = ny * nz * CORES
    kb = hd // parts
    rows = nx * slots
    half = 2 * ny
    plane = ny * nz
    cols = xin.shape[2]
    admitted = admit_ref.shape[0]
    wide = parts * admitted * kb

    x = lax.axis_index("sec")
    ep = lax.axis_index("ep")
    c = lax.rem(ep, CORES)
    z = lax.rem(ep // CORES, nz)
    y = ep // (CORES * nz)

    here = x * ny + y
    place_yz = y * nz + z

    def at(xx, yy, zz, cc):
        return (xx, (yy * nz + zz) * CORES + cc)

    def remote(src, dst, send_sem, recv_sem, device):
        return pltpu.make_async_remote_copy(
            src, dst, send_sem, recv_sem, device_id=device, device_id_type=MESH
        )

    def step(start, by, size):
        return lax.rem(start + by, size)

    other = at(x, y, z, 1 - c)
    in_plane = [(step(y, dy, ny), step(z, dz, nz)) for dy, dz in far_first(ny, nz)]
    in_column = [step(z, dz, nz) for (dz,) in far_first(nz)]
    in_row = [step(x, dx, nx) for (dx,) in far_first(nx)]
    steps_xy = far_first(nx, ny)

    def all_of(src, dst, send_sem, recv_sem):
        count = plane - 1
        return remote(
            src.at[pl.ds(0, count)], dst.at[pl.ds(0, count)], send_sem, recv_sem, other
        )

    incoming_hbm, *others = operands
    held = (
        admit_ref,
        occupancy_ref,
        q_ref,
        k_ref,
        v_ref,
        decay_ref,
        state_v,
        routes_ref,
        weight_ref,
        residual_ref,
        wo_v,
        gain_ref,
        gate_v,
        up_v,
        down_v,
    )
    incoming_loads = [
        pltpu.make_async_copy(
            incoming_hbm.at[a], incoming_v.at[:, kb * a : kb * (a + 1), :], local_sem.at[a]
        )
        for a in range(admitted)
    ]
    loads = [
        pltpu.make_async_copy(src, dst, local_sem.at[admitted + i])
        for i, (src, dst) in enumerate(zip(others, held))
    ]
    for load in incoming_loads + loads:
        load.start()

    barrier = pltpu.get_barrier_semaphore()
    partners = [at(x, yy, zz, c) for yy, zz in in_plane] + [other]
    partners += [
        at(step(x, dx, nx), step(y, dy, ny), z, c) for dx, dy in far_first(nx, ny) if dx
    ]
    for partner in partners:
        pl.semaphore_signal(barrier, inc=1, device_id=partner, device_id_type=MESH)

    for load in incoming_loads:
        load.wait()
    blocks = incoming_v[...].astype(BF16)
    snd1[...] = blocks.reshape(plane, CORES, admitted * kb, hd)
    pl.semaphore_wait(barrier, len(partners))
    copy0 = remote(snd1.at[:, 1 - c], pair1.at[:, c], s0.at[0], r0.at[0], other)
    copy0.start()
    pair1[:, c] = snd1[:, c]
    copy0.wait_recv()
    for yy, zz in in_plane:
        remote(
            pair1.at[yy * nz + zz],
            rcv1.at[place_yz],
            s1.at[0],
            r1.at[0],
            at(x, yy, zz, c),
        ).start()
    rcv1[place_yz] = pair1[place_yz]
    every1 = all_of(pair1, rcv1, s1.at[0], r1.at[0])

    for load in loads[:7]:
        load.wait()

    q = q_ref[...].astype(F32)
    kk = k_ref[...].astype(F32)
    vv = v_ref[...].astype(F32)
    occupancy = occupancy_ref[...].astype(F32)
    eye = iota((slots, slots), 0) == iota((slots, slots), 1)
    kept = jnp.sum(jnp.where(eye, occupancy, 0.0), axis=1, keepdims=True)
    slot_row = iota((slots, 1), 0)
    taken = jnp.zeros((slots, 1), jnp.bool_)
    lane = iota((1, wide), 1)
    lane_request = (lane // kb) % admitted
    lane_slot = jnp.zeros((1, wide), jnp.int32)
    for a in range(admitted):
        slot = admit_ref[a] - x * slots
        taken = jnp.logical_or(taken, slot_row == slot)
        lane_slot = jnp.where(lane_request == a, slot, lane_slot)
    old_q = jnp.where(taken, 0.0, q * kept)
    lane2 = iota((hd, wide), 1)
    spread_key = (lane2 // (admitted * kb)) * kb + lane2 % kb
    repeat = (iota((hd, wide), 0) == spread_key).astype(BF16)
    new_q = dot(q.astype(BF16), repeat)
    new_q = jnp.where(slot_row == lane_slot, new_q, 0.0).astype(BF16)
    base_old = []
    row8 = iota((8, hd), 0)
    for chunk in range(slots // 8):
        part = old_q[chunk * 8 : chunk * 8 + 8]
        diagonal = jnp.concatenate(
            [jnp.where(row8 == s, part, 0.0) for s in range(8)], axis=1
        ).astype(BF16)
        states = state_v[chunk * 8 * hd : (chunk + 1) * 8 * hd, :].astype(BF16)
        base_old.append(dot(diagonal, states))
    for load in loads[7:9]:
        load.wait()

    position0 = iota((rows, rows), 0)
    position1 = iota((rows, rows), 1)
    row_of0 = natural_row(position0, grid)
    row_of1 = natural_row(position1, grid)
    to_held = (position0 == row_of1).astype(F32)
    not_after = (row_of0 <= row_of1).astype(BF16)
    expert = iota((8, rows), 0) * (nz // 2) + z // 2
    hit = jnp.zeros((8, rows), jnp.bool_)
    weight = jnp.zeros((8, rows), F32)
    for t in range(routes_ref.shape[0]):
        route = jnp.broadcast_to(routes_ref[t : t + 1, :].astype(F32), (8, rows))
        route = dot(route.astype(BF16), to_held.astype(BF16))
        gate_value = jnp.broadcast_to(weight_ref[t : t + 1, :], (8, rows))
        gate_value = dot(gate_value, to_held, precision=lax.Precision.HIGHEST)
        same = route == expert.astype(F32)
        hit = jnp.logical_or(hit, same)
        weight = weight + jnp.where(same, gate_value, 0.0)
    rank = dot(hit.astype(F32).astype(BF16), not_after)
    rank = jnp.where(hit, rank, 0.0)
    place = (iota((CAPACITY, rows), 0) + 1).astype(F32)
    picks, slot_weights = [], []
    for yy in range(ny):
        chosen = rank[yy : yy + 1, :] == place
        picks.append(chosen.astype(F32))
        slot_weights.append(
            jnp.sum(jnp.where(chosen, weight[yy : yy + 1, :], 0.0), axis=1, keepdims=True)
        )
    pick = jnp.concatenate(picks, axis=0).astype(BF16)
    from_held = (position1 == row_of0).astype(BF16)

    every1.wait_recv()
    arrived = rcv1[...].astype(F32).reshape(wide, hd).astype(BF16)
    base = jnp.concatenate(base_old, axis=0) + dot(new_q, arrived)
    raw = jnp.exp(-decay_ref[...]) * base + jnp.sum(q * kk, axis=1, keepdims=True) * vv
    power = jnp.mean(raw * raw, axis=1, keepdims=True)
    heads_buf[x] = (raw * lax.rsqrt(power + EPSILON)).astype(BF16)

    copies2 = []
    for i, xx in enumerate(in_row):
        copy = remote(heads_buf.at[x], heads_buf.at[x], s2.at[i], r2.at[i], at(xx, y, z, c))
        copy.start()
        copies2.append(copy)
    for load in loads[9:12]:
        load.wait()
    for copy in copies2:
        copy.wait_recv()

    heads = heads_buf[...].reshape(rows, hd)
    heads = dot(from_held, heads).astype(BF16)
    row_in_half = iota((half, cols), 0)
    copies3 = []
    for yy in range(ny):
        product = dot(heads, wo_v[:, yy * cols : (yy + 1) * cols])
        partial[yy] = product.reshape(nz, CORES, half, cols)
        res = residual_ref[:, yy * cols : (yy + 1) * cols].astype(F32)
        partial[yy, z, c] += jnp.where(row_in_half == 2 * y, res[0:1, :], 0.0) + jnp.where(
            row_in_half == 2 * y + 1, res[1:2, :], 0.0
        )
        snd3[yy] = partial[yy, :, 1 - c].astype(BF16)
        copy = remote(snd3.at[yy], rcv3.at[yy], s3.at[yy], r3.at[yy], other)
        copy.start()
        copies3.append(copy)

    for yy in range(ny):
        copies3[yy].wait_recv()
        for zz in range(nz):
            snd4[yy * nz + zz] = (partial[yy, zz, c] + rcv3[yy, zz].astype(F32)).astype(BF16)
    for i, (yy, zz) in enumerate(in_plane):
        remote(
            snd4.at[yy * nz + zz], rcv4.at[i], s4.at[0], r4.at[0], at(x, yy, zz, c)
        ).start()
    mine = partial[y, z, c] + rcv3[y, z].astype(F32)
    every4 = all_of(snd4, rcv4, s4.at[0], r4.at[0])
    every4.wait_recv()
    for i in range(plane - 1):
        mine = mine + rcv4[i].astype(F32)
    mixed = mine.astype(BF16)

    full[z, c] = mixed
    copy5 = remote(full.at[z, c], full.at[z, c], s5.at[0], r5.at[0], other)
    copy5.start()
    copy5.wait_recv()
    copies6 = []
    for i, zz in enumerate(in_column):
        copy = remote(full.at[z], full.at[z], s6.at[i], r6.at[i], at(x, y, zz, c))
        copy.start()
        copies6.append(copy)
    for copy in copies6:
        copy.wait_recv()

    every_row = full[...].astype(F32).reshape(rows, cols).astype(BF16)
    picked = dot(pick, every_row).astype(BF16)
    for yy in range(ny):
        snd7[yy] = picked[yy * CAPACITY : (yy + 1) * CAPACITY]
    copies7 = []
    for i, (dx, dy) in enumerate(steps_xy):
        xx, yy = step(x, dx, nx), step(y, dy, ny)
        copy = remote(snd7.at[yy], xin.at[here], s7.at[i], r7.at[i], at(xx, yy, z, c))
        copy.start()
        copies7.append(copy)
    xin[here] = snd7[y]
    for load in loads[12:]:
        load.wait()

    def one_block(block, carry):
        gate_sum, up_sum, squares = carry
        taken_rows = xin[block].astype(F32)
        columns = pl.ds(pl.multiple_of(block * cols, cols), cols)
        squares = squares + jnp.sum(taken_rows * taken_rows, axis=1, keepdims=True)
        scaled = (taken_rows * gain_ref[:, columns]).astype(BF16)
        gate_sum = gate_sum + dot(scaled, gate_v[:, columns], ((1,), (1,)))
        up_sum = up_sum + dot(scaled, up_v[:, columns], ((1,), (1,)))
        return gate_sum, up_sum, squares

    hidden_units = gate_v.shape[0]
    carry = (
        jnp.zeros((CAPACITY, hidden_units), F32),
        jnp.zeros((CAPACITY, hidden_units), F32),
        jnp.zeros((CAPACITY, 1), F32),
    )
    carry = one_block(here, carry)
    for i in reversed(range(nx * ny - 1)):
        dx, dy = steps_xy[i]
        copies7[i].wait_recv()
        carry = one_block(step(x, nx - dx, nx) * ny + step(y, ny - dy, ny), carry)
    gate_sum, up_sum, squares = carry
    scale = lax.rsqrt(squares / (nx * ny * cols) + EPSILON)
    gate_sum = gate_sum * scale
    up_sum = up_sum * scale
    hidden = (gate_sum / (1.0 + jnp.exp(-gate_sum)) * up_sum).astype(BF16)

    def down_block(block):
        columns = pl.ds(pl.multiple_of(block * cols, cols), cols)
        return dot(hidden, down_v[:, columns]).astype(BF16)

    copies8 = []
    for i, (dx, dy) in enumerate(steps_xy):
        xx, yy = step(x, dx, nx), step(y, dy, ny)
        snd8[i] = down_block(xx * ny + yy)
        copy = remote(snd8.at[i], rcv8.at[here], s8.at[i], r8.at[i], at(xx, yy, z, c))
        copy.start()
        copies8.append(copy)
    rcv8[here] = down_block(here)
    for copy in copies8:
        copy.wait_recv()

    summed = []
    for yy in range(ny):
        term = rcv8[yy].astype(F32)
        for xx in range(1, nx):
            term = term + rcv8[xx * ny + yy].astype(F32)
        summed.append(term * slot_weights[yy])
    summed = jnp.concatenate(summed, axis=0).astype(BF16)
    routed = dot(pick, summed, ((0,), (0,)))
    own9[...] = routed.reshape(nz, CORES, half, cols)

    snd9[...] = own9[:, 1 - c].astype(BF16)
    copy9 = remote(snd9, rcv9, s9.at[0], r9.at[0], other)
    copy9.start()
    own9[z, c] += mixed.astype(F32)
    copy9.wait_recv()
    for zz in range(nz):
        block = own9[zz, c] + rcv9[zz].astype(F32)
        for yy in range(ny):
            snd10[yy * nz + zz] = block[2 * yy : 2 * yy + 2, :]
    for yy, zz in in_plane:
        remote(
            snd10.at[yy * nz + zz],
            rcv10.at[place_yz],
            s10.at[0],
            r10.at[0],
            at(x, yy, zz, c),
        ).start()
    rcv10[place_yz] = snd10[place_yz]
    every10 = all_of(snd10, rcv10, s10.at[0], r10.at[0])
    every10.wait_recv()
    for yy in range(ny):
        total = rcv10[yy * nz]
        for zz in range(1, nz):
            total = total + rcv10[yy * nz + zz]
        out_ref[:, yy * cols : (yy + 1) * cols] = total.astype(BF16)

    for copy in [copy0, every1, every4, copy5, copy9, every10]:
        copy.wait_send()
    for copy in copies2 + copies3 + copies6 + copies7 + copies8:
        copy.wait_send()


def body(
    grid,
    residual_in,
    queries,
    keys_new,
    values_new,
    cached_state,
    incoming_state,
    admit_slot,
    occupancy,
    decay_rate,
    out_proj,
    norm_gain,
    routes,
    route_weight,
    gate_proj,
    up_proj,
    down_proj,
):
    nx, ny, nz = grid
    slots, hd = queries.shape
    rows = nx * slots
    half = 2 * ny
    plane = ny * nz
    cols = residual_in.shape[1] // ny
    blocks = nx * ny
    units = gate_proj.shape[2]
    width = gate_proj.shape[1]
    admitted, parts, kb, _ = incoming_state.shape

    vmem = pl.BlockSpec(memory_space=pltpu.VMEM)
    anywhere = pl.BlockSpec(memory_space=pl.ANY)
    dma = lambda n: pltpu.SemaphoreType.DMA((n,))
    scratch = [
        pltpu.VMEM((parts, admitted * kb, hd), F32),
        pltpu.SMEM(admit_slot.shape, jnp.int32),
        pltpu.VMEM((1, slots), jnp.int32),
        pltpu.VMEM((slots, hd), BF16),
        pltpu.VMEM((slots, hd), BF16),
        pltpu.VMEM((slots, hd), BF16),
        pltpu.VMEM((1, 1), F32),
        pltpu.VMEM((routes.shape[1], rows), jnp.int32),
        pltpu.VMEM((routes.shape[1], rows), F32),
        pltpu.VMEM(residual_in.shape, BF16),
        pltpu.VMEM((1, width), F32),
        pltpu.VMEM((slots * hd, hd), F32),
        pltpu.VMEM(out_proj.shape, BF16),
        pltpu.VMEM((units, width), BF16),
        pltpu.VMEM((units, width), BF16),
        pltpu.VMEM((units, width), BF16),
        pltpu.VMEM((plane, CORES, admitted * kb, hd), BF16),
        pltpu.VMEM((plane, CORES, admitted * kb, hd), BF16),
        pltpu.VMEM((plane, CORES, admitted * kb, hd), BF16),
        pltpu.VMEM((nx, slots, hd), BF16),
        pltpu.VMEM((ny, nz, CORES, half, cols), F32),
        pltpu.VMEM((ny, nz, half, cols), BF16),
        pltpu.VMEM((ny, nz, half, cols), BF16),
        pltpu.VMEM((plane, half, cols), BF16),
        pltpu.VMEM((plane, half, cols), BF16),
        pltpu.VMEM((nz, CORES, half, cols), BF16),
        pltpu.VMEM((ny, CAPACITY, cols), BF16),
        pltpu.VMEM((blocks, CAPACITY, cols), BF16),
        pltpu.VMEM((blocks, CAPACITY, cols), BF16),
        pltpu.VMEM((blocks, CAPACITY, cols), BF16),
        pltpu.VMEM((nz, CORES, half, cols), F32),
        pltpu.VMEM((nz, half, cols), BF16),
        pltpu.VMEM((nz, half, cols), BF16),
        pltpu.VMEM((plane, 2, cols), F32),
        pltpu.VMEM((plane, 2, cols), F32),
        dma(admitted + 15),
    ]
    for n in (1, 1, nx - 1, ny, 1, 1, nz - 1, blocks - 1, blocks - 1, 1, 1):
        scratch += [dma(n), dma(n)]

    def kernel(*refs):
        layer_kernel(grid, refs[:16], *refs[16:])

    return pl.pallas_call(
        kernel,
        out_shape=jax.ShapeDtypeStruct(residual_in.shape, BF16),
        in_specs=[anywhere] * 16,
        out_specs=vmem,
        scratch_shapes=scratch,
        compiler_params=pltpu.CompilerParams(
            collective_id=0, has_side_effects=True, vmem_limit_bytes=VMEM_BYTES
        ),
    )(
        incoming_state,
        admit_slot,
        occupancy.reshape(1, slots),
        queries,
        keys_new,
        values_new,
        decay_rate.reshape(1, 1),
        cached_state.reshape(slots * hd, hd),
        routes.T,
        route_weight.T,
        residual_in,
        out_proj,
        norm_gain.reshape(1, width),
        gate_proj[0].T,
        up_proj[0].T,
        down_proj[0],
    )


def solution(mesh):
    in_specs = (
        P("ep", "sec"),
        P("sec", "ep"),
        P("sec", "ep"),
        P("sec", "ep"),
        P("sec", "ep", None, None),
        P("sec", None, "ep", None),
        P("sec"),
        P("sec"),
        P("ep"),
        P("ep", "sec"),
        P(),
        P(),
        P(),
        P("ep", None, "sec"),
        P("ep", None, "sec"),
        P("ep", "sec", None),
    )
    return jax.shard_map(
        functools.partial(body, GRID),
        mesh=mesh,
        in_specs=in_specs,
        out_specs=P("ep", "sec"),
        check_vma=False,
    )
```

time: 73.8 us -> 65.2 us (0.88)
  Pallas kernels: 71.7 us -> 63.1 us
    pallas_call x1, Pallas kernels: 71.7 us -> 63.1 us  [body(): pl.pallas_call(kernel, out_shape=jax.ShapeDtypeStruct(residual_in.shape,...]
where the time goes in v3:
time: 65.2 us; the launch traced here: 65 us
  Pallas kernels  63.1 us (97%)
  local copies, waits for them, and re-layouts  1.29 us (2%)
  between operations  0.66 us (1%)
    pallas_call x1, Pallas kernels, body(): pl.pallas_call(kernel, out_shape=jax.ShapeDtypeStruct(residual_in.shape,...  63.1 us

profile of v3, /device:TPU:1, one launch (start us, length us, event | category | flops | bytes accessed | tf_op | source)
XLA Modules:
  0.0 65.0 jit_solution(7071615573743946113)
XLA Ops:
  0.7 63.1 %shard_map.154 = bf16[2,1536]{1,0:T(2,128)(2,1)} custom-call(f32[4,64,2,128]{3,2,1,0:T(2,128)} %refs_0_.1, s32[4]{0:T(128)} %refs_1_.1, s32[1,32]{1,0:T(1,128)} %bitcast.21, bf16[32,128]{1,0:T(8,128)(2,1)} %refs_3_.1, bf16[32,128]{1,0:T(8,128)(2,1)} %refs_4_.1, bf16[32,128]{1,0:T(8,128)(2,1)} %refs_5_.1, f32[1,1]{1,0:T(1,128)} %bitcast.13.refs_6_, ...), custom_call_target="tpu_custom_call" | custom-call | tf_op jit(solution)/shard_map/pallas_call | solution.py:514
  63.7 1.3 %copy.19 = bf16[2,1536]{1,0:T(2,128)(2,1)} copy(bf16[2,1536]{1,0:T(2,128)(2,1)} %shard_map.154) | data formatting | bytes 12288

commit v4 on v3

--- a/solution.py
+++ b/solution.py
@@ -70,8 +70,6 @@
     rcv1,
     heads_buf,
     partial,
-    snd3,
-    rcv3,
     snd4,
     rcv4,
     full,
@@ -142,7 +140,7 @@
     other = at(x, y, z, 1 - c)
     in_plane = [(step(y, dy, ny), step(z, dz, nz)) for dy, dz in far_first(ny, nz)]
     in_column = [step(z, dz, nz) for (dz,) in far_first(nz)]
-    in_row = [step(x, dx, nx) for (dx,) in far_first(nx)]
+    in_row = [(step(x, dx, nx), step(c, dc, CORES)) for dx, dc in far_first(nx, CORES)]
     steps_xy = far_first(nx, ny)
 
     def all_of(src, dst, send_sem, recv_sem):
@@ -163,7 +161,7 @@
         routes_ref,
         weight_ref,
         residual_ref,
-        wo_v,
+        wo_v.at[c],
         gain_ref,
         gate_v,
         up_v,
@@ -187,6 +185,7 @@
     partners += [
         at(step(x, dx, nx), step(y, dy, ny), z, c) for dx, dy in far_first(nx, ny) if dx
     ]
+    partners += [at(xx, y, z, 1 - c) for xx in [step(x, dx, nx) for dx in range(1, nx)]]
     for partner in partners:
         pl.semaphore_signal(barrier, inc=1, device_id=partner, device_id_type=MESH)
 
@@ -198,6 +197,9 @@
     copy0 = remote(snd1.at[:, 1 - c], pair1.at[:, c], s0.at[0], r0.at[0], other)
     copy0.start()
     pair1[:, c] = snd1[:, c]
+    wo_hbm = others[10]
+    copy_wo = remote(wo_hbm, wo_v.at[c], s3.at[0], r3.at[0], other)
+    copy_wo.start()
     copy0.wait_recv()
     for yy, zz in in_plane:
         remote(
@@ -274,50 +276,51 @@
             jnp.sum(jnp.where(chosen, weight[yy : yy + 1, :], 0.0), axis=1, keepdims=True)
         )
     pick = jnp.concatenate(picks, axis=0).astype(BF16)
-    from_held = (position1 == row_of0).astype(BF16)
+    mine0 = iota((rows // CORES, rows), 0)
+    mine0 = (mine0 // half) * (CORES * half) + c * half + mine0 % half
+    mine0 = natural_row(mine0, grid)
+    from_held = (iota((rows // CORES, rows), 1) == mine0).astype(BF16)
 
     every1.wait_recv()
     arrived = rcv1[...].astype(F32).reshape(wide, hd).astype(BF16)
     base = jnp.concatenate(base_old, axis=0) + dot(new_q, arrived)
     raw = jnp.exp(-decay_ref[...]) * base + jnp.sum(q * kk, axis=1, keepdims=True) * vv
     power = jnp.mean(raw * raw, axis=1, keepdims=True)
-    heads_buf[x] = (raw * lax.rsqrt(power + EPSILON)).astype(BF16)
+    heads_buf[c, x] = (raw * lax.rsqrt(power + EPSILON)).astype(BF16)
 
     copies2 = []
-    for i, xx in enumerate(in_row):
-        copy = remote(heads_buf.at[x], heads_buf.at[x], s2.at[i], r2.at[i], at(xx, y, z, c))
+    for i, (xx, cc) in enumerate(in_row):
+        copy = remote(
+            heads_buf.at[c, x], heads_buf.at[c, x], s2.at[i], r2.at[i], at(xx, y, z, cc)
+        )
         copy.start()
         copies2.append(copy)
     for load in loads[9:12]:
         load.wait()
+    copy_wo.wait_recv()
     for copy in copies2:
         copy.wait_recv()
 
-    heads = heads_buf[...].reshape(rows, hd)
-    heads = dot(from_held, heads).astype(BF16)
+    heads = jnp.concatenate(
+        [dot(from_held, heads_buf[cc].reshape(rows, hd)).astype(BF16) for cc in range(CORES)],
+        axis=1,
+    )
     row_in_half = iota((half, cols), 0)
-    copies3 = []
     for yy in range(ny):
-        product = dot(heads, wo_v[:, yy * cols : (yy + 1) * cols])
-        partial[yy] = product.reshape(nz, CORES, half, cols)
-        res = residual_ref[:, yy * cols : (yy + 1) * cols].astype(F32)
-        partial[yy, z, c] += jnp.where(row_in_half == 2 * y, res[0:1, :], 0.0) + jnp.where(
+        columns = slice(yy * cols, (yy + 1) * cols)
+        weights = wo_v[:, :, columns].reshape(CORES * hd, cols)
+        partial[yy] = dot(heads, weights).reshape(nz, half, cols)
+        res = residual_ref[:, columns].astype(F32)
+        partial[yy, z] += jnp.where(row_in_half == 2 * y, res[0:1, :], 0.0) + jnp.where(
             row_in_half == 2 * y + 1, res[1:2, :], 0.0
         )
-        snd3[yy] = partial[yy, :, 1 - c].astype(BF16)
-        copy = remote(snd3.at[yy], rcv3.at[yy], s3.at[yy], r3.at[yy], other)
-        copy.start()
-        copies3.append(copy)
-
-    for yy in range(ny):
-        copies3[yy].wait_recv()
-        for zz in range(nz):
-            snd4[yy * nz + zz] = (partial[yy, zz, c] + rcv3[yy, zz].astype(F32)).astype(BF16)
+        snd4[yy * nz : (yy + 1) * nz] = partial[yy].astype(BF16)
+
     for i, (yy, zz) in enumerate(in_plane):
         remote(
             snd4.at[yy * nz + zz], rcv4.at[i], s4.at[0], r4.at[0], at(x, yy, zz, c)
         ).start()
-    mine = partial[y, z, c] + rcv3[y, z].astype(F32)
+    mine = partial[y, z]
     every4 = all_of(snd4, rcv4, s4.at[0], r4.at[0])
     every4.wait_recv()
     for i in range(plane - 1):
@@ -428,9 +431,9 @@
             total = total + rcv10[yy * nz + zz]
         out_ref[:, yy * cols : (yy + 1) * cols] = total.astype(BF16)
 
-    for copy in [copy0, every1, every4, copy5, copy9, every10]:
+    for copy in [copy0, copy_wo, every1, every4, copy5, copy9, every10]:
         copy.wait_send()
-    for copy in copies2 + copies3 + copies6 + copies7 + copies8:
+    for copy in copies2 + copies6 + copies7 + copies8:
         copy.wait_send()
 
 
@@ -480,17 +483,15 @@
         pltpu.VMEM(residual_in.shape, BF16),
         pltpu.VMEM((1, width), F32),
         pltpu.VMEM((slots * hd, hd), F32),
-        pltpu.VMEM(out_proj.shape, BF16),
+        pltpu.VMEM((CORES,) + out_proj.shape, BF16),
         pltpu.VMEM((units, width), BF16),
         pltpu.VMEM((units, width), BF16),
         pltpu.VMEM((units, width), BF16),
         pltpu.VMEM((plane, CORES, admitted * kb, hd), BF16),
         pltpu.VMEM((plane, CORES, admitted * kb, hd), BF16),
         pltpu.VMEM((plane, CORES, admitted * kb, hd), BF16),
-        pltpu.VMEM((nx, slots, hd), BF16),
-        pltpu.VMEM((ny, nz, CORES, half, cols), F32),
-        pltpu.VMEM((ny, nz, half, cols), BF16),
-        pltpu.VMEM((ny, nz, half, cols), BF16),
+        pltpu.VMEM((CORES, nx, slots, hd), BF16),
+        pltpu.VMEM((ny, nz, half, cols), F32),
         pltpu.VMEM((plane, half, cols), BF16),
         pltpu.VMEM((plane, half, cols), BF16),
         pltpu.VMEM((nz, CORES, half, cols), BF16),
@@ -505,7 +506,7 @@
         pltpu.VMEM((plane, 2, cols), F32),
         dma(admitted + 15),
     ]
-    for n in (1, 1, nx - 1, ny, 1, 1, nz - 1, blocks - 1, blocks - 1, 1, 1):
+    for n in (1, 1, nx * CORES - 1, 1, 1, 1, nz - 1, blocks - 1, blocks - 1, 1, 1):
         scratch += [dma(n), dma(n)]
 
     def kernel(*refs):
@@ -513,7 +514,7 @@
 
     return pl.pallas_call(
         kernel,
-        out_shape=jax.ShapeDtypeStruct(residual_in.shape, BF16),
+        out_shape=pltpu.VMEM(residual_in.shape, BF16),
         in_specs=[anywhere] * 16,
         out_specs=vmem,
         scratch_shapes=scratch,

time: 65.2 us -> 62.6 us (0.960)
  Pallas kernels: 63.1 us -> 61.2 us
  local copies, waits for them, and re-layouts: 1.29 us -> 0.6 us
    pallas_call x1, Pallas kernels: 63.1 us -> 61.2 us  [body(): pl.pallas_call(kernel, out_shape=pltpu.VMEM(residual_in.shape, BF16), in_...]
    unnamed x1, local copies, waits for them, and re-layouts: 1.29 us -> 0.6 us
where the time goes in v4:
time: 62.6 us; the launch traced here: 62.5 us
  Pallas kernels  61.2 us (98%)
  between operations  0.66 us (1%)
    pallas_call x1, Pallas kernels, body(): pl.pallas_call(kernel, out_shape=pltpu.VMEM(residual_in.shape, BF16), in_...  61.2 us

profile of v4, /device:TPU:1, one launch (start us, length us, event | category | flops | bytes accessed | tf_op | source)
XLA Modules:
  0.0 62.5 jit_solution(2252391684666855299)
XLA Ops:
  0.7 61.2 %shard_map.154 = bf16[2,1536]{1,0:T(2,128)(2,1)S(1)} custom-call(f32[4,64,2,128]{3,2,1,0:T(2,128)} %refs_0_.1, s32[4]{0:T(128)} %refs_1_.1, s32[1,32]{1,0:T(1,128)} %bitcast.21, bf16[32,128]{1,0:T(8,128)(2,1)} %refs_3_.1, bf16[32,128]{1,0:T(8,128)(2,1)} %refs_4_.1, bf16[32,128]{1,0:T(8,128)(2,1)} %refs_5_.1, f32[1,1]{1,0:T(1,128)} %bitcast.13.refs_6_, ...), custom_call_target="tpu_custom_call" | custom-call | tf_op jit(solution)/shard_map/pallas_call | solution.py:515
  61.9 0.6 copy.18

commit v5 on v4

--- a/solution.py
+++ b/solution.py
@@ -69,7 +69,8 @@
     pair1,
     rcv1,
     heads_buf,
-    partial,
+    residual_buf,
+    summed8,
     snd4,
     rcv4,
     full,
@@ -83,6 +84,8 @@
     snd10,
     rcv10,
     local_sem,
+    s_res,
+    r_res,
     s0,
     r0,
     s1,
@@ -177,7 +180,7 @@
         pltpu.make_async_copy(src, dst, local_sem.at[admitted + i])
         for i, (src, dst) in enumerate(zip(others, held))
     ]
-    for load in incoming_loads + loads:
+    for load in incoming_loads:
         load.start()
 
     barrier = pltpu.get_barrier_semaphore()
@@ -188,6 +191,8 @@
     partners += [at(xx, y, z, 1 - c) for xx in [step(x, dx, nx) for dx in range(1, nx)]]
     for partner in partners:
         pl.semaphore_signal(barrier, inc=1, device_id=partner, device_id_type=MESH)
+    for load in loads:
+        load.start()
 
     for load in incoming_loads:
         load.wait()
@@ -211,6 +216,22 @@
         ).start()
     rcv1[place_yz] = pair1[place_yz]
     every1 = all_of(pair1, rcv1, s1.at[0], r1.at[0])
+
+    loads[9].wait()
+    copies_res = []
+    for i, (dy,) in enumerate(far_first(ny)):
+        yy = step(y, dy, ny)
+        columns = pl.ds(pl.multiple_of(yy * cols, cols), cols)
+        copy = remote(
+            residual_ref.at[:, columns],
+            residual_buf.at[y],
+            s_res.at[i],
+            r_res.at[i],
+            at(x, yy, z, c),
+        )
+        copy.start()
+        copies_res.append(copy)
+    residual_buf[y] = residual_ref[:, pl.ds(pl.multiple_of(y * cols, cols), cols)]
 
     for load in loads[:7]:
         load.wait()
@@ -245,6 +266,10 @@
         ).astype(BF16)
         states = state_v[chunk * 8 * hd : (chunk + 1) * 8 * hd, :].astype(BF16)
         base_old.append(dot(diagonal, states))
+    decay = jnp.exp(-decay_ref[...])
+    old_part = decay * jnp.concatenate(base_old, axis=0)
+    old_part = old_part + jnp.sum(q * kk, axis=1, keepdims=True) * vv
+
     for load in loads[7:9]:
         load.wait()
 
@@ -275,7 +300,9 @@
         slot_weights.append(
             jnp.sum(jnp.where(chosen, weight[yy : yy + 1, :], 0.0), axis=1, keepdims=True)
         )
-    pick = jnp.concatenate(picks, axis=0).astype(BF16)
+    pick = jnp.concatenate(picks, axis=0)
+    place_rows = pick.T.astype(BF16)
+    pick = pick.astype(BF16)
     mine0 = iota((rows // CORES, rows), 0)
     mine0 = (mine0 // half) * (CORES * half) + c * half + mine0 % half
     mine0 = natural_row(mine0, grid)
@@ -283,8 +310,7 @@
 
     every1.wait_recv()
     arrived = rcv1[...].astype(F32).reshape(wide, hd).astype(BF16)
-    base = jnp.concatenate(base_old, axis=0) + dot(new_q, arrived)
-    raw = jnp.exp(-decay_ref[...]) * base + jnp.sum(q * kk, axis=1, keepdims=True) * vv
+    raw = old_part + decay * dot(new_q, arrived)
     power = jnp.mean(raw * raw, axis=1, keepdims=True)
     heads_buf[c, x] = (raw * lax.rsqrt(power + EPSILON)).astype(BF16)
 
@@ -295,7 +321,7 @@
         )
         copy.start()
         copies2.append(copy)
-    for load in loads[9:12]:
+    for load in loads[10:12]:
         load.wait()
     copy_wo.wait_recv()
     for copy in copies2:
@@ -305,23 +331,23 @@
         [dot(from_held, heads_buf[cc].reshape(rows, hd)).astype(BF16) for cc in range(CORES)],
         axis=1,
     )
-    row_in_half = iota((half, cols), 0)
     for yy in range(ny):
-        columns = slice(yy * cols, (yy + 1) * cols)
-        weights = wo_v[:, :, columns].reshape(CORES * hd, cols)
-        partial[yy] = dot(heads, weights).reshape(nz, half, cols)
-        res = residual_ref[:, columns].astype(F32)
-        partial[yy, z] += jnp.where(row_in_half == 2 * y, res[0:1, :], 0.0) + jnp.where(
-            row_in_half == 2 * y + 1, res[1:2, :], 0.0
-        )
-        snd4[yy * nz : (yy + 1) * nz] = partial[yy].astype(BF16)
+        weights = wo_v[:, :, yy * cols : (yy + 1) * cols].reshape(CORES * hd, cols)
+        product = dot(heads, weights).astype(BF16)
+        snd4[yy * nz : (yy + 1) * nz] = product.reshape(nz, half, cols)
 
     for i, (yy, zz) in enumerate(in_plane):
         remote(
             snd4.at[yy * nz + zz], rcv4.at[i], s4.at[0], r4.at[0], at(x, yy, zz, c)
         ).start()
-    mine = partial[y, z]
     every4 = all_of(snd4, rcv4, s4.at[0], r4.at[0])
+    for copy in copies_res:
+        copy.wait_recv()
+    mine = snd4[place_yz].astype(F32) + jnp.concatenate(
+        [residual_buf[yy].astype(F32) for yy in range(ny)], axis=0
+    )
+    for copy in [copy0, copy_wo, every1] + copies2 + copies_res:
+        copy.wait_send()
     every4.wait_recv()
     for i in range(plane - 1):
         mine = mine + rcv4[i].astype(F32)
@@ -336,6 +362,8 @@
         copy = remote(full.at[z], full.at[z], s6.at[i], r6.at[i], at(x, y, zz, c))
         copy.start()
         copies6.append(copy)
+    for copy in [every4, copy5]:
+        copy.wait_send()
     for copy in copies6:
         copy.wait_recv()
 
@@ -350,6 +378,8 @@
         copy.start()
         copies7.append(copy)
     xin[here] = snd7[y]
+    for copy in copies6:
+        copy.wait_send()
     for load in loads[12:]:
         load.wait()
 
@@ -391,18 +421,21 @@
         copy = remote(snd8.at[i], rcv8.at[here], s8.at[i], r8.at[i], at(xx, yy, z, c))
         copy.start()
         copies8.append(copy)
-    rcv8[here] = down_block(here)
-    for copy in copies8:
-        copy.wait_recv()
-
-    summed = []
-    for yy in range(ny):
-        term = rcv8[yy].astype(F32)
-        for xx in range(1, nx):
-            term = term + rcv8[xx * ny + yy].astype(F32)
-        summed.append(term * slot_weights[yy])
+    block = dot(hidden, down_v[:, pl.ds(pl.multiple_of(here * cols, cols), cols)])
+    for yy in range(1, ny):
+        summed8[step(y, yy, ny)] = jnp.zeros(block.shape, F32)
+    summed8[y] = block
+    for copy in copies7:
+        copy.wait_send()
+    for i in reversed(range(nx * ny - 1)):
+        dx, dy = steps_xy[i]
+        xx, yy = step(x, nx - dx, nx), step(y, ny - dy, ny)
+        copies8[i].wait_recv()
+        summed8[yy] += rcv8[xx * ny + yy].astype(F32)
+
+    summed = [summed8[yy] * slot_weights[yy] for yy in range(ny)]
     summed = jnp.concatenate(summed, axis=0).astype(BF16)
-    routed = dot(pick, summed, ((0,), (0,)))
+    routed = dot(place_rows, summed)
     own9[...] = routed.reshape(nz, CORES, half, cols)
 
     snd9[...] = own9[:, 1 - c].astype(BF16)
@@ -424,6 +457,8 @@
         ).start()
     rcv10[place_yz] = snd10[place_yz]
     every10 = all_of(snd10, rcv10, s10.at[0], r10.at[0])
+    for copy in copies8 + [copy9]:
+        copy.wait_send()
     every10.wait_recv()
     for yy in range(ny):
         total = rcv10[yy * nz]
@@ -431,10 +466,7 @@
             total = total + rcv10[yy * nz + zz]
         out_ref[:, yy * cols : (yy + 1) * cols] = total.astype(BF16)
 
-    for copy in [copy0, copy_wo, every1, every4, copy5, copy9, every10]:
-        copy.wait_send()
-    for copy in copies2 + copies6 + copies7 + copies8:
-        copy.wait_send()
+    every10.wait_send()
 
 
 def body(
@@ -491,7 +523,8 @@
         pltpu.VMEM((plane, CORES, admitted * kb, hd), BF16),
         pltpu.VMEM((plane, CORES, admitted * kb, hd), BF16),
         pltpu.VMEM((CORES, nx, slots, hd), BF16),
-        pltpu.VMEM((ny, nz, half, cols), F32),
+        pltpu.VMEM((ny, 2, cols), BF16),
+        pltpu.VMEM((ny, CAPACITY, cols), F32),
         pltpu.VMEM((plane, half, cols), BF16),
         pltpu.VMEM((plane, half, cols), BF16),
         pltpu.VMEM((nz, CORES, half, cols), BF16),
@@ -506,7 +539,7 @@
         pltpu.VMEM((plane, 2, cols), F32),
         dma(admitted + 15),
     ]
-    for n in (1, 1, nx * CORES - 1, 1, 1, 1, nz - 1, blocks - 1, blocks - 1, 1, 1):
+    for n in (ny - 1, 1, 1, nx * CORES - 1, 1, 1, 1, nz - 1, blocks - 1, blocks - 1, 1, 1):
         scratch += [dma(n), dma(n)]
 
     def kernel(*refs):

time: 62.6 us -> 62.9 us (level)
  no operation moved by 1% of the time
where the time goes in v5:
time: 62.9 us; the launch traced here: 62.8 us
  Pallas kernels  61.6 us (98%)
  between operations  0.66 us (1%)
    pallas_call x1, Pallas kernels, body(): pl.pallas_call(kernel, out_shape=pltpu.VMEM(residual_in.shape, BF16), in_...  61.6 us

profile of v5, /device:TPU:1, one launch (start us, length us, event | category | flops | bytes accessed | tf_op | source)
XLA Modules:
  0.0 62.8 jit_solution(18373223133479035240)
XLA Ops:
  0.7 61.6 %shard_map.154 = bf16[2,1536]{1,0:T(2,128)(2,1)S(1)} custom-call(f32[4,64,2,128]{3,2,1,0:T(2,128)} %refs_0_.1, s32[4]{0:T(128)} %refs_1_.1, s32[1,32]{1,0:T(1,128)} %bitcast.21, bf16[32,128]{1,0:T(8,128)(2,1)} %refs_3_.1, bf16[32,128]{1,0:T(8,128)(2,1)} %refs_4_.1, bf16[32,128]{1,0:T(8,128)(2,1)} %refs_5_.1, f32[1,1]{1,0:T(1,128)} %bitcast.13.refs_6_, ...), custom_call_target="tpu_custom_call" | custom-call | tf_op jit(solution)/shard_map/pallas_call | solution.py:548
  62.2 0.6 copy.18

commit v6 on v4

--- a/solution.py
+++ b/solution.py
@@ -66,7 +66,6 @@
     up_v,
     down_v,
     snd1,
-    pair1,
     rcv1,
     heads_buf,
     partial,
@@ -83,8 +82,6 @@
     snd10,
     rcv10,
     local_sem,
-    s0,
-    r0,
     s1,
     r1,
     s2,
@@ -93,8 +90,6 @@
     r3,
     s4,
     r4,
-    s5,
-    r5,
     s6,
     r6,
     s7,
@@ -138,8 +133,12 @@
         return lax.rem(start + by, size)
 
     other = at(x, y, z, 1 - c)
+    in_ep = [
+        (step(y, dy, ny), step(z, dz, nz), step(c, dc, CORES))
+        for dy, dz, dc in far_first(ny, nz, CORES)
+    ]
     in_plane = [(step(y, dy, ny), step(z, dz, nz)) for dy, dz in far_first(ny, nz)]
-    in_column = [step(z, dz, nz) for (dz,) in far_first(nz)]
+    in_column = [(step(z, dz, nz), step(c, dc, CORES)) for dz, dc in far_first(nz, CORES)]
     in_row = [(step(x, dx, nx), step(c, dc, CORES)) for dx, dc in far_first(nx, CORES)]
     steps_xy = far_first(nx, ny)
 
@@ -181,7 +180,7 @@
         load.start()
 
     barrier = pltpu.get_barrier_semaphore()
-    partners = [at(x, yy, zz, c) for yy, zz in in_plane] + [other]
+    partners = [at(x, yy, zz, cc) for yy, zz, cc in in_ep]
     partners += [
         at(step(x, dx, nx), step(y, dy, ny), z, c) for dx, dy in far_first(nx, ny) if dx
     ]
@@ -191,26 +190,27 @@
 
     for load in incoming_loads:
         load.wait()
-    blocks = incoming_v[...].astype(BF16)
-    snd1[...] = blocks.reshape(plane, CORES, admitted * kb, hd)
+    snd1[...] = incoming_v[...].astype(BF16)
     pl.semaphore_wait(barrier, len(partners))
-    copy0 = remote(snd1.at[:, 1 - c], pair1.at[:, c], s0.at[0], r0.at[0], other)
-    copy0.start()
-    pair1[:, c] = snd1[:, c]
     wo_hbm = others[10]
     copy_wo = remote(wo_hbm, wo_v.at[c], s3.at[0], r3.at[0], other)
-    copy_wo.start()
-    copy0.wait_recv()
-    for yy, zz in in_plane:
+    for yy, zz, cc in in_ep:
         remote(
-            pair1.at[yy * nz + zz],
-            rcv1.at[place_yz],
+            snd1.at[(yy * nz + zz) * CORES + cc],
+            rcv1.at[ep],
             s1.at[0],
             r1.at[0],
-            at(x, yy, zz, c),
+            at(x, yy, zz, cc),
         ).start()
-    rcv1[place_yz] = pair1[place_yz]
-    every1 = all_of(pair1, rcv1, s1.at[0], r1.at[0])
+    rcv1[ep] = snd1[ep]
+    copy_wo.start()
+    every1 = remote(
+        snd1.at[pl.ds(0, parts - 1)],
+        rcv1.at[pl.ds(0, parts - 1)],
+        s1.at[0],
+        r1.at[0],
+        other,
+    )
 
     for load in loads[:7]:
         load.wait()
@@ -328,12 +328,9 @@
     mixed = mine.astype(BF16)
 
     full[z, c] = mixed
-    copy5 = remote(full.at[z, c], full.at[z, c], s5.at[0], r5.at[0], other)
-    copy5.start()
-    copy5.wait_recv()
     copies6 = []
-    for i, zz in enumerate(in_column):
-        copy = remote(full.at[z], full.at[z], s6.at[i], r6.at[i], at(x, y, zz, c))
+    for i, (zz, cc) in enumerate(in_column):
+        copy = remote(full.at[z, c], full.at[z, c], s6.at[i], r6.at[i], at(x, y, zz, cc))
         copy.start()
         copies6.append(copy)
     for copy in copies6:
@@ -431,7 +428,7 @@
             total = total + rcv10[yy * nz + zz]
         out_ref[:, yy * cols : (yy + 1) * cols] = total.astype(BF16)
 
-    for copy in [copy0, copy_wo, every1, every4, copy5, copy9, every10]:
+    for copy in [copy_wo, every1, every4, copy9, every10]:
         copy.wait_send()
     for copy in copies2 + copies6 + copies7 + copies8:
         copy.wait_send()
@@ -487,9 +484,8 @@
         pltpu.VMEM((units, width), BF16),
         pltpu.VMEM((units, width), BF16),
         pltpu.VMEM((units, width), BF16),
-        pltpu.VMEM((plane, CORES, admitted * kb, hd), BF16),
-        pltpu.VMEM((plane, CORES, admitted * kb, hd), BF16),
-        pltpu.VMEM((plane, CORES, admitted * kb, hd), BF16),
+        pltpu.VMEM((parts, admitted * kb, hd), BF16),
+        pltpu.VMEM((parts, admitted * kb, hd), BF16),
         pltpu.VMEM((CORES, nx, slots, hd), BF16),
         pltpu.VMEM((ny, nz, half, cols), F32),
         pltpu.VMEM((plane, half, cols), BF16),
@@ -506,7 +502,7 @@
         pltpu.VMEM((plane, 2, cols), F32),
         dma(admitted + 15),
     ]
-    for n in (1, 1, nx * CORES - 1, 1, 1, 1, nz - 1, blocks - 1, blocks - 1, 1, 1):
+    for n in (1, nx * CORES - 1, 1, 1, nz * CORES - 1, blocks - 1, blocks - 1, 1, 1):
         scratch += [dma(n), dma(n)]
 
     def kernel(*refs):

time: 62.6 us -> 61.9 us (0.989)
  Pallas kernels: 61.2 us -> 60.5 us
    pallas_call x1, Pallas kernels: 61.2 us -> 60.5 us  [body(): pl.pallas_call(kernel, out_shape=pltpu.VMEM(residual_in.shape, BF16), in_...]
where the time goes in v6:
time: 61.9 us; the launch traced here: 61.8 us
  Pallas kernels  60.5 us (98%)
  between operations  0.66 us (1%)
    pallas_call x1, Pallas kernels, body(): pl.pallas_call(kernel, out_shape=pltpu.VMEM(residual_in.shape, BF16), in_...  60.5 us

profile of v6, /device:TPU:1, one launch (start us, length us, event | category | flops | bytes accessed | tf_op | source)
XLA Modules:
  0.0 61.8 jit_solution(8048732896324558975)
XLA Ops:
  0.7 60.5 %shard_map.154 = bf16[2,1536]{1,0:T(2,128)(2,1)S(1)} custom-call(f32[4,64,2,128]{3,2,1,0:T(2,128)} %refs_0_.1, s32[4]{0:T(128)} %refs_1_.1, s32[1,32]{1,0:T(1,128)} %bitcast.21, bf16[32,128]{1,0:T(8,128)(2,1)} %refs_3_.1, bf16[32,128]{1,0:T(8,128)(2,1)} %refs_4_.1, bf16[32,128]{1,0:T(8,128)(2,1)} %refs_5_.1, f32[1,1]{1,0:T(1,128)} %bitcast.13.refs_6_, ...), custom_call_target="tpu_custom_call" | custom-call | tf_op jit(solution)/shard_map/pallas_call | solution.py:511
  61.2 0.6 copy.18

commit v7 on v6

--- a/solution.py
+++ b/solution.py
@@ -65,6 +65,8 @@
     gate_v,
     up_v,
     down_v,
+    gate_t,
+    up_t,
     snd1,
     rcv1,
     heads_buf,
@@ -72,6 +74,7 @@
     snd4,
     rcv4,
     full,
+    pick_buf,
     snd7,
     xin,
     snd8,
@@ -276,6 +279,8 @@
             jnp.sum(jnp.where(chosen, weight[yy : yy + 1, :], 0.0), axis=1, keepdims=True)
         )
     pick = jnp.concatenate(picks, axis=0).astype(BF16)
+    for yy in range(ny):
+        pick_buf[yy] = picks[yy].astype(BF16)
     mine0 = iota((rows // CORES, rows), 0)
     mine0 = (mine0 // half) * (CORES * half) + c * half + mine0 % half
     mine0 = natural_row(mine0, grid)
@@ -322,6 +327,12 @@
         ).start()
     mine = partial[y, z]
     every4 = all_of(snd4, rcv4, s4.at[0], r4.at[0])
+    for load in loads[12:14]:
+        load.wait()
+    for block in range(nx * ny):
+        columns = slice(block * cols, (block + 1) * cols)
+        gate_t[columns, :] = gate_v[:, columns].T
+        up_t[columns, :] = up_v[:, columns].T
     every4.wait_recv()
     for i in range(plane - 1):
         mine = mine + rcv4[i].astype(F32)
@@ -337,18 +348,25 @@
         copy.wait_recv()
 
     every_row = full[...].astype(F32).reshape(rows, cols).astype(BF16)
-    picked = dot(pick, every_row).astype(BF16)
-    for yy in range(ny):
-        snd7[yy] = picked[yy * CAPACITY : (yy + 1) * CAPACITY]
+    for dy in [dy for (dy,) in far_first(ny)] + [0]:
+        yy = step(y, dy, ny)
+        snd7[yy] = dot(pick_buf[yy], every_row).astype(BF16)
+        for i, (dx, dyy) in enumerate(steps_xy):
+            if dyy == dy:
+                remote(
+                    snd7.at[yy],
+                    xin.at[here],
+                    s7.at[i],
+                    r7.at[i],
+                    at(step(x, dx, nx), yy, z, c),
+                ).start()
     copies7 = []
     for i, (dx, dy) in enumerate(steps_xy):
         xx, yy = step(x, dx, nx), step(y, dy, ny)
         copy = remote(snd7.at[yy], xin.at[here], s7.at[i], r7.at[i], at(xx, yy, z, c))
-        copy.start()
         copies7.append(copy)
     xin[here] = snd7[y]
-    for load in loads[12:]:
-        load.wait()
+    loads[14].wait()
 
     def one_block(block, carry):
         gate_sum, up_sum, squares = carry
@@ -356,8 +374,8 @@
         columns = pl.ds(pl.multiple_of(block * cols, cols), cols)
         squares = squares + jnp.sum(taken_rows * taken_rows, axis=1, keepdims=True)
         scaled = (taken_rows * gain_ref[:, columns]).astype(BF16)
-        gate_sum = gate_sum + dot(scaled, gate_v[:, columns], ((1,), (1,)))
-        up_sum = up_sum + dot(scaled, up_v[:, columns], ((1,), (1,)))
+        gate_sum = gate_sum + dot(scaled, gate_t[columns, :])
+        up_sum = up_sum + dot(scaled, up_t[columns, :])
         return gate_sum, up_sum, squares
 
     hidden_units = gate_v.shape[0]
@@ -367,7 +385,7 @@
         jnp.zeros((CAPACITY, 1), F32),
     )
     carry = one_block(here, carry)
-    for i in reversed(range(nx * ny - 1)):
+    for i in range(nx * ny - 1):
         dx, dy = steps_xy[i]
         copies7[i].wait_recv()
         carry = one_block(step(x, nx - dx, nx) * ny + step(y, ny - dy, ny), carry)
@@ -484,6 +502,8 @@
         pltpu.VMEM((units, width), BF16),
         pltpu.VMEM((units, width), BF16),
         pltpu.VMEM((units, width), BF16),
+        pltpu.VMEM((width, units), BF16),
+        pltpu.VMEM((width, units), BF16),
         pltpu.VMEM((parts, admitted * kb, hd), BF16),
         pltpu.VMEM((parts, admitted * kb, hd), BF16),
         pltpu.VMEM((CORES, nx, slots, hd), BF16),
@@ -491,6 +511,7 @@
         pltpu.VMEM((plane, half, cols), BF16),
         pltpu.VMEM((plane, half, cols), BF16),
         pltpu.VMEM((nz, CORES, half, cols), BF16),
+        pltpu.VMEM((ny, CAPACITY, rows), BF16),
         pltpu.VMEM((ny, CAPACITY, cols), BF16),
         pltpu.VMEM((blocks, CAPACITY, cols), BF16),
         pltpu.VMEM((blocks, CAPACITY, cols), BF16),

time: 61.9 us -> 59.3 us (0.958)
  Pallas kernels: 60.5 us -> 58 us
    pallas_call x1, Pallas kernels: 60.5 us -> 58 us  [body(): pl.pallas_call(kernel, out_shape=pltpu.VMEM(residual_in.shape, BF16), in_...]
where the time goes in v7:
time: 59.3 us
  Pallas kernels  58 us (98%)
  between operations  0.66 us (1%)
  local copies, waits for them, and re-layouts  0.6 us (1%)
    pallas_call x1, Pallas kernels, body(): pl.pallas_call(kernel, out_shape=pltpu.VMEM(residual_in.shape, BF16), in_...  58 us

profile of v7, /device:TPU:1, one launch (start us, length us, event | category | flops | bytes accessed | tf_op | source)
XLA Modules:
  0.0 59.3 jit_solution(10960748268375303474)
XLA Ops:
  0.7 58.0 %shard_map.154 = bf16[2,1536]{1,0:T(2,128)(2,1)S(1)} custom-call(f32[4,64,2,128]{3,2,1,0:T(2,128)} %refs_0_.1, s32[4]{0:T(128)} %refs_1_.1, s32[1,32]{1,0:T(1,128)} %bitcast.21, bf16[32,128]{1,0:T(8,128)(2,1)} %refs_3_.1, bf16[32,128]{1,0:T(8,128)(2,1)} %refs_4_.1, bf16[32,128]{1,0:T(8,128)(2,1)} %refs_5_.1, f32[1,1]{1,0:T(1,128)} %bitcast.13.refs_6_, ...), custom_call_target="tpu_custom_call" | custom-call | tf_op jit(solution)/shard_map/pallas_call | solution.py:532
  58.7 0.6 %copy.18 = bf16[2,1536]{1,0:T(2,128)(2,1)} copy(bf16[2,1536]{1,0:T(2,128)(2,1)S(1)} %shard_map.154) | data formatting | bytes 12288

commit v8 on v7

--- a/solution.py
+++ b/solution.py
@@ -143,7 +143,7 @@
     in_plane = [(step(y, dy, ny), step(z, dz, nz)) for dy, dz in far_first(ny, nz)]
     in_column = [(step(z, dz, nz), step(c, dc, CORES)) for dz, dc in far_first(nz, CORES)]
     in_row = [(step(x, dx, nx), step(c, dc, CORES)) for dx, dc in far_first(nx, CORES)]
-    steps_xy = far_first(nx, ny)
+    steps_xy = sorted(far_first(nx, ny), key=lambda d: -(min(d[0], nx - d[0]) + 2 * min(d[1], ny - d[1])))
 
     def all_of(src, dst, send_sem, recv_sem):
         count = plane - 1

time: 59.3 us -> 59.1 us (level)
  no operation moved by 1% of the time
where the time goes in v8:
time: 59.1 us; the launch traced here: 59 us
  Pallas kernels  57.8 us (98%)
  between operations  0.66 us (1%)
  local copies, waits for them, and re-layouts  0.6 us (1%)
    pallas_call x1, Pallas kernels, body(): pl.pallas_call(kernel, out_shape=pltpu.VMEM(residual_in.shape, BF16), in_...  57.8 us

profile of v8, /device:TPU:1, one launch (start us, length us, event | category | flops | bytes accessed | tf_op | source)
XLA Modules:
  0.0 59.0 jit_solution(3797453506467904559)
XLA Ops:
  0.7 57.8 %shard_map.154 = bf16[2,1536]{1,0:T(2,128)(2,1)S(1)} custom-call(f32[4,64,2,128]{3,2,1,0:T(2,128)} %refs_0_.1, s32[4]{0:T(128)} %refs_1_.1, s32[1,32]{1,0:T(1,128)} %bitcast.21, bf16[32,128]{1,0:T(8,128)(2,1)} %refs_3_.1, bf16[32,128]{1,0:T(8,128)(2,1)} %refs_4_.1, bf16[32,128]{1,0:T(8,128)(2,1)} %refs_5_.1, f32[1,1]{1,0:T(1,128)} %bitcast.13.refs_6_, ...), custom_call_target="tpu_custom_call" | custom-call | tf_op jit(solution)/shard_map/pallas_call | solution.py:532
  58.4 0.6 %copy.18 = bf16[2,1536]{1,0:T(2,128)(2,1)} copy(bf16[2,1536]{1,0:T(2,128)(2,1)S(1)} %shard_map.154) | data formatting | bytes 12288
